TPU v7x, 256 devices: a whole 4x4x8 slice. The times are simulated.
256 devices in a mesh: dom: 16 (over y, z_hi), row: 16 (over x, z_lo, core).
Axes of the slice: x: 4, y: 4, z: 8 (z_hi: 4, z_lo: 2; z = z_hi * 2 + z_lo), core: 2. Of those that a mesh axis runs over, the one named last changes fastest.
Arguments:
- left_emb: float32 [32768, 400], P(('dom', 'row')), may hold values from -1.5 to 1.5
- left_state: float32 [32768], P(('dom', 'row')), may hold values from 0.05 to 1
- right_emb: float32 [32768, 400], P(('dom', 'row')), may hold values from -1.5 to 1.5
- right_state: float32 [32768], P(('dom', 'row')), may hold values from 0.05 to 1
- rel_diag: float32 [16, 400], replicated, may hold values from -4 to 4
- edge_src: int32 [2, 262144], P(None, ('dom', 'row')), may hold values from 0 to 2047
- edge_rel: int32 [2, 262144], P(None, ('dom', 'row')), may hold values from 0 to 15
- edge_dst: int32 [2, 262144], P(None, ('dom', 'row')), may hold values from 0 to 2047
- neg_rows: int32 [2, 256, 128], P(None, ('dom', 'row')), may hold values from 0 to 2047
Outputs:
- left_table: float32 [32768, 400], P(('dom', 'row'))
- left_accum: float32 [32768], P(('dom', 'row'))
- right_table: float32 [32768, 400], P(('dom', 'row'))
- right_accum: float32 [32768], P(('dom', 'row'))
- relation_grad: float32 [16, 400], replicated
All inputs are finite; a program needn't handle non-finite values.
Results may differ from a plain program's by a relative error of at most 0.0021.
Values may be sent and summed in bfloat16 or wider, within the bound.
A program may use at most 64 MiB of HBM per device.

v0:
```python
import jax
import jax.numpy as jnp
from jax import lax
from jax.sharding import PartitionSpec as P

ROUNDS = 2


STEP_SIZE = 0.1
EPSILON = 1e-10


def swapped(value, axis, stride):
    mask = 2**stride
    pairs = [(source, source ^ mask) for source in range(lax.axis_size(axis))]
    return lax.ppermute(value, axis, pairs)


def pick_rows(totals, piece, index):
    row_count = piece.shape[0]
    inside = (index >= 0) & (index < row_count)
    rows = jnp.take(piece, jnp.clip(index, 0, row_count - 1), axis=0)
    return jnp.where(inside[:, None], rows, totals)


def grad_term(values, index, row_count):
    inside = (index >= 0) & (index < row_count)
    clipped = jnp.clip(index, 0, row_count - 1)
    masked = jnp.where(inside[:, None], values, 0.0)
    return jnp.zeros((row_count, values.shape[1]), jnp.float32).at[clipped].add(masked)


def adagrad(rows_in, state_in, grad_in):
    new_state = state_in + jnp.mean(grad_in * grad_in, axis=-1)
    return (rows_in - STEP_SIZE * grad_in / (jnp.sqrt(new_state)[:, None] + EPSILON), new_state)


def span_terms(left_rows, right_rows, neg_block, rel_rows, neg_count):
    span_len = left_rows.shape[0]
    block_len = min(512, span_len)
    anchor = (left_rows.astype(jnp.float32) * rel_rows).astype(jnp.bfloat16)
    column_ids = jnp.arange(span_len, dtype=jnp.int32)
    grad_dst = jnp.zeros(right_rows.shape, jnp.float32)
    grad_neg = jnp.zeros(neg_block.shape, jnp.float32)
    anchor_parts = []
    for block_idx in range(span_len // block_len):
        anchor_block = anchor[block_idx * block_len : (block_idx + 1) * block_len]
        inner_scores = lax.dot_general(
            anchor_block, right_rows, (((1,), (1,)), ((), ())), preferred_element_type=jnp.float32
        )
        outer_scores = lax.dot_general(
            anchor_block, neg_block, (((1,), (1,)), ((), ())), preferred_element_type=jnp.float32
        )
        row_ids = block_idx * block_len + jnp.arange(block_len, dtype=jnp.int32)
        on_diag = row_ids[:, None] == column_ids[None, :]
        w_inner = jnp.where(
            on_diag, -jax.nn.sigmoid(-inner_scores), jax.nn.sigmoid(inner_scores) / neg_count
        ).astype(jnp.bfloat16)
        w_outer = (jax.nn.sigmoid(outer_scores) / neg_count).astype(jnp.bfloat16)
        anchor_parts.append(
            jnp.dot(w_inner, right_rows, preferred_element_type=jnp.float32)
            + jnp.dot(w_outer, neg_block, preferred_element_type=jnp.float32)
        )
        grad_dst = grad_dst + lax.dot_general(
            w_inner, anchor_block, (((0,), (0,)), ((), ())), preferred_element_type=jnp.float32
        )
        grad_neg = grad_neg + lax.dot_general(
            w_outer, anchor_block, (((0,), (0,)), ((), ())), preferred_element_type=jnp.float32
        )
    return (jnp.concatenate(anchor_parts, axis=0), grad_dst, grad_neg)


def per_device(
    left_emb, left_state, right_emb, right_state, rel_diag, edge_src, edge_rel, edge_dst, neg_rows
):
    rows_dev, model_width = left_emb.shape
    edges_dev = edge_src.shape[1]
    span_count = neg_rows.shape[1]
    uniform_len = neg_rows.shape[2]
    span_len = edges_dev // span_count
    rel_count = rel_diag.shape[0]
    neg_count = span_len - 1 + uniform_len
    swap_bit = lax.axis_size("dom").bit_length() - 2
    device_count = lax.axis_size("dom") * lax.axis_size("row")
    rel_total = jnp.zeros((rel_count, model_width), jnp.float32)
    rel_iota = jnp.arange(rel_count, dtype=jnp.int32)
    for round_idx in range(ROUNDS):
        left_low = left_emb.astype(jnp.bfloat16)
        right_low = right_emb.astype(jnp.bfloat16)
        sources = edge_src[round_idx]
        targets = edge_dst[round_idx]
        rel_ids = edge_rel[round_idx]
        right_index = jnp.concatenate([targets, neg_rows[round_idx].reshape(-1)])
        left_start = jnp.zeros((edges_dev, model_width), jnp.bfloat16)
        right_start = jnp.zeros((right_index.shape[0], model_width), jnp.bfloat16)
        left_rows = pick_rows(
            left_start, lax.all_gather(left_low, "row", axis=0, tiled=True), sources
        )
        right_rows = pick_rows(
            right_start, lax.all_gather(right_low, "row", axis=0, tiled=True), right_index
        )
        onehot = (rel_ids[:, None] == rel_iota[None, :]).astype(jnp.float32)
        rel_rows = jnp.dot(onehot, rel_diag, precision=lax.Precision.HIGHEST)
        grad_anchor, grad_dst, grad_neg = span_terms(
            left_rows,
            right_rows[0:span_len],
            right_rows[edges_dev : edges_dev + uniform_len],
            rel_rows,
            neg_count,
        )
        anchor_grads = grad_anchor
        dst_grads = [grad_dst]
        neg_grads = [grad_neg]
        grad_anchor = anchor_grads
        grad_src = grad_anchor * rel_rows
        right_values = jnp.concatenate(dst_grads + neg_grads, axis=0)
        rel_term = jnp.dot(
            onehot.T, grad_anchor * left_rows.astype(jnp.float32), precision=lax.Precision.HIGHEST
        )
        left_grad = lax.psum_scatter(
            grad_term(grad_src, sources, rows_dev * lax.axis_size("row")),
            "row",
            scatter_dimension=0,
            tiled=True,
        )
        right_grad = lax.psum_scatter(
            grad_term(right_values, right_index, rows_dev * lax.axis_size("row")),
            "row",
            scatter_dimension=0,
            tiled=True,
        )
        left_emb, left_state = adagrad(left_emb, left_state, left_grad)
        new_rows, new_state = adagrad(right_emb, right_state, right_grad)
        right_emb, right_state = swapped((new_rows, new_state), "dom", swap_bit)
        rel_total = rel_total + lax.psum(rel_term, ("dom", "row"))
    relation_grad = rel_total * (ROUNDS * edges_dev * device_count) ** (-0.5)
    return (left_emb, left_state, right_emb, right_state, relation_grad)


def solution(mesh):
    placed = (
        P(("dom", "row"), None),
        P(("dom", "row")),
        P(("dom", "row"), None),
        P(("dom", "row")),
        P(),
        P(None, ("dom", "row")),
        P(None, ("dom", "row")),
        P(None, ("dom", "row")),
        P(None, ("dom", "row"), None),
    )
    return jax.shard_map(
        per_device,
        mesh=mesh,
        in_specs=placed,
        out_specs=(
            P(("dom", "row"), None),
            P(("dom", "row")),
            P(("dom", "row"), None),
            P(("dom", "row")),
            P(),
        ),
        check_vma=False,
    )
```

profile of v0, /device:TPU:24, one launch (start us, length us, event | category | flops | bytes accessed | tf_op | source)
XLA Modules:
  0.0 527.3 jit_solution(3862587248073963783)
XLA Ops:
  7.2 1.6 convert_element_type.55
  8.9 1.6 convert_element_type.52
  10.6 1.2 slice_bitcast_fusion
  11.8 1.4 slice_bitcast_fusion.4
  13.2 1.4 and_reduce_fusion
  14.6 0.8 slice_clamp_fusion
  15.4 1.4 compare_select_fusion.3
  16.8 0.8 fusion.118
  17.6 34.0 %all-gather.7.cloned.1.call-done = bf16[2048,400]{0,1:T(8,128)(2,1)} async-done(((bf16[128,400]{0,1:T(8,128)(2,1)}), bf16[2048,400]{0,1:T(8,128)(2,1)}) %all-gather.7.cloned.1.call-update) | async-done | bytes 1638416 | tf_op jit(solution)/shard_map/all_gather | solution.py:100
  51.6 2.8 copy.42
  54.4 4.2 gather_fusion.1
  58.6 1.5 copy.43
  60.1 32.3 %all-gather.5.cloned.1.call-done = bf16[2048,400]{0,1:T(8,128)(2,1)} async-done(((bf16[128,400]{0,1:T(8,128)(2,1)}), bf16[2048,400]{0,1:T(8,128)(2,1)}) %all-gather.5.cloned.1.call-update) | async-done | bytes 1638416 | tf_op jit(solution)/shard_map/all_gather | solution.py:97
  92.4 2.8 copy.40
  95.1 4.0 gather_fusion
  99.6 0.7 copy-done.9
  100.5 1.2 fusion.8
  102.4 1.1 select_convert_fusion.3
  104.1 1.6 select_convert_fusion.2
  105.6 0.6 convolution_add_fusion.4
  107.2 0.7 copy-done.16
  108.3 1.8 copy.44
  110.1 9.9 %scatter_custom_fusion = f32[2048,400]{1,0:T(8,128)} fusion(s32[1024]{0:T(1024)} %bitcast.55, f32[1024,400]{1,0:T(8,128)} %copy.44, f32[]{:T(128)} %constant.16.clone.1), kind=kCustom, calls=%fused_computation.20 | custom fusion | flops 409600 | bytes 3277312 | tf_op jit(solution)/shard_map/scatter-add | solution.py:30
  123.2 2.0 copy.47
  125.2 12.5 %scatter_custom_fusion.1 = f32[2048,400]{1,0:T(8,128)} fusion(s32[1152]{0:T(1024)S(1)} %fusion.107, f32[1152,400]{1,0:T(8,128)} %copy.47, f32[]{:T(128)} %constant.16.clone.1), kind=kCustom, calls=%fused_computation.18 | custom fusion | flops 460800 | bytes 3277312 | tf_op jit(solution)/shard_map/scatter-add | solution.py:30
  137.8 0.8 copy-done.25
  138.8 53.2 %reduce-scatter.5.cloned.1.call-done = f32[128,400]{1,0:T(8,128)} async-done(((f32[2048,400]{1,0:T(8,128)}), f32[128,400]{1,0:T(8,128)}) %reduce-scatter.5.cloned.1.call-update) | async-done | bytes 204816 | tf_op jit(solution)/shard_map/reduce_scatter | solution.py:120
  192.0 1.1 multiply_reduce_fusion.3
  193.1 1.7 fusion.117
  195.0 70.1 %reduce-scatter.7.cloned.1.call-done = f32[128,400]{1,0:T(8,128)} async-done(((f32[2048,400]{1,0:T(8,128)}), f32[128,400]{1,0:T(8,128)}) %reduce-scatter.7.cloned.1.call-update) | async-done | bytes 204816 | tf_op jit(solution)/shard_map/reduce_scatter | solution.py:126
  265.1 1.1 multiply_reduce_fusion.2
  266.2 1.0 divide_subtract_fusion.2
  267.2 1.4 collective-permute-start
  268.7 6.5 %collective-permute-done = f32[128,400]{1,0:T(8,128)S(1)} collective-permute-done((f32[128,400]{1,0:T(8,128)S(1)}, f32[128,400]{1,0:T(8,128)S(1)}, u32[]{:S(2)}, u32[]{:S(2)}) %collective-permute-start) | collective-permute-done | bytes 204832 | tf_op jit(solution)/shard_map/ppermute | solution.py:16
  275.2 0.7 copy-done.23
  275.9 0.7 convert_element_type.63
  277.0 25.2 %all-gather.9.cloned.1.call-done = bf16[2048,400]{1,0:T(8,128)(2,1)} async-done(((bf16[128,400]{1,0:T(8,128)(2,1)}), bf16[2048,400]{1,0:T(8,128)(2,1)}) %all-gather.9.cloned.1.call-update) | async-done | bytes 1638416 | tf_op jit(solution)/shard_map/all_gather | solution.py:97
  302.1 5.8 %gather_fusion.2 = bf16[1024,400]{1,0:T(8,128)(2,1)S(1)} fusion(bf16[2048,400]{1,0:T(8,128)(2,1)} %all-gather.9.cloned.1.call-done, s32[1024]{0:T(1024)S(1)} %fusion.110), kind=kCustom, calls=%fused_computation.2.clone | custom fusion | bytes 1642496 | tf_op jit(solution)/shard_map/jit(_take)/gather | solution.py:22
  308.5 2.4 fusion.10
  310.9 29.9 %all-gather.11.cloned.1.call-done = bf16[2048,400]{1,0:T(8,128)(2,1)} async-done(((bf16[128,400]{1,0:T(8,128)(2,1)}), bf16[2048,400]{1,0:T(8,128)(2,1)}) %all-gather.11.cloned.1.call-update) | async-done | bytes 1638416 | tf_op jit(solution)/shard_map/all_gather | solution.py:100
  340.9 6.2 %gather_fusion.3 = bf16[1152,400]{1,0:T(8,128)(2,1)S(1)} fusion(bf16[2048,400]{1,0:T(8,128)(2,1)} %all-gather.11.cloned.1.call-done, s32[2048]{0:T(1024)S(1)} %pad_clamp_fusion), kind=kCustom, calls=%fused_computation.3.clone | custom fusion | bytes 1847808 | tf_op jit(solution)/shard_map/jit(_take)/gather | solution.py:22
  347.0 1.5 copy.49
  348.5 1.3 select_select_fusion
  350.6 1.6 select_convert_fusion
  352.2 1.1 select_convert_fusion.1
  355.2 2.0 copy.51
  357.3 12.6 %scatter_custom_fusion.3 = f32[2048,400]{1,0:T(8,128)} fusion(s32[1152]{0:T(1024)S(1)} %fusion.108, f32[1152,400]{1,0:T(8,128)} %copy.51, f32[]{:T(128)} %constant.16.clone.1), kind=kCustom, calls=%fused_computation.14 | custom fusion | flops 460800 | bytes 3277312 | tf_op jit(solution)/shard_map/scatter-add | solution.py:30
  372.4 0.8 copy-done.2
  373.6 1.9 copy.50
  375.4 9.5 %scatter_custom_fusion.2 = f32[2048,400]{1,0:T(8,128)} fusion(s32[1024]{0:T(1024)} %bitcast.54, f32[1024,400]{1,0:T(8,128)} %copy.50, f32[]{:T(128)} %constant.16.clone.1), kind=kCustom, calls=%fused_computation.16 | custom fusion | flops 409600 | bytes 3277312 | tf_op jit(solution)/shard_map/scatter-add | solution.py:30
  385.0 1.1 copy-done.11
  386.6 1.2 fusion.9
  387.8 1.5 collective-permute-start.1
  389.4 1.2 fusion.32
  390.6 77.5 %psum.16 = f32[16,400]{1,0:T(8,128)S(1)} all-reduce(f32[16,400]{1,0:T(8,128)S(1)} %fusion.32), channel_id=1, replica_groups=mesh['dom'=16,'row'=16] {'dom','row'}, use_global_device_ids=true, to_apply=%region_12.15 | all-reduce | flops 6400 | bytes 51200 | tf_op jit(solution)/shard_map/psum | solution.py:135
  468.7 1.1 multiply_reduce_fusion
  469.8 1.5 collective-permute-start.3
  471.4 1.1 divide_subtract_fusion
  472.4 2.2 collective-permute-start.2
  474.6 40.8 %reduce-scatter.9.cloned.1.call-done = f32[128,400]{1,0:T(8,128)} async-done(((f32[2048,400]{1,0:T(8,128)}), f32[128,400]{1,0:T(8,128)}) %reduce-scatter.9.cloned.1.call-update) | async-done | bytes 204816 | tf_op jit(solution)/shard_map/reduce_scatter | solution.py:120
  515.4 1.1 multiply_reduce_fusion.1
  517.0 1.1 divide_subtract_fusion.1
  518.1 0.8 copy.52
  518.9 0.8 copy.53
  (157 shorter events, 15.3 us)
Async XLA Ops:
  7.2 93.3 %copy-start = (f32[16,400]{1,0:T(8,128)S(1)}, f32[16,400]{1,0:T(8,128)}, u32[]{:S(2)}) copy-start(f32[16,400]{1,0:T(8,128)} %param.17) | copy-start | bytes 76804
  7.2 44.4 %all-gather.7.cloned.1.call-start = ((), (), s32[]{:S(2)}) async-start(), calls=%async_computation.5 | async-start | bytes 1740800 | tf_op jit(solution)/shard_map/all_gather | solution.py:100
  8.8 83.5 %all-gather.5.cloned.1.call-start = ((), (), s32[]{:S(2)}) async-start(), calls=%async_computation.4 | async-start | bytes 1740800 | tf_op jit(solution)/shard_map/all_gather | solution.py:97
  10.5 181.5 %reduce-scatter.5.cloned.1.call-start = ((), (), s32[]{:S(2)}) async-start(), calls=%async_computation.6 | async-start | bytes 4456448 | tf_op jit(solution)/shard_map/reduce_scatter | solution.py:120
  10.6 93.5 %copy-start.42 = (s32[512]{0:T(512)}, s32[512]{0:T(512)S(1)}, u32[]{:S(2)}) copy-start(s32[512]{0:T(512)S(1)} %iota_add_fusion) | copy-start | bytes 6148
  14.6 85.8 %copy-start.36 = (pred[1024]{0:T(1024)(128)(4,1)}, pred[1024]{0:T(1024)(128)(4,1)S(1)}, u32[]{:S(2)}) copy-start(pred[1024]{0:T(1024)(128)(4,1)S(1)} %get-tuple-element.23) | copy-start | bytes 3076
  15.4 85.0 %copy-start.40 = (pred[1024]{0:T(1024)(128)(4,1)}, pred[1024]{0:T(1024)(128)(4,1)S(1)}, u32[]{:S(2)}) copy-start(pred[1024]{0:T(1024)(128)(4,1)S(1)} %compare_and_fusion.3) | copy-start | bytes 3076
  17.6 82.9 %copy-start.31 = (s32[1,1024]{1,0:T(1,128)}, s32[1,1024]{1,0:T(1,128)S(1)}, u32[]{:S(2)}) copy-start(s32[1,1024]{1,0:T(1,128)S(1)} %get-tuple-element.36) | copy-start | bytes 12292
  99.1 1.2 copy-start.9
  99.6 2.0 copy-start.10
  102.0 1.8 copy-start.27
  102.4 1.1 copy-start.29
  105.6 1.3 copy-start.5
  106.3 0.9 copy-start.14
  106.3 1.6 copy-start.37
  107.0 1.0 copy-start.16
  120.0 0.7 copy-start.34
  120.0 0.7 copy-start.45
  120.0 0.9 copy-start.28
  120.0 1.2 copy-start.30
  120.1 145.0 %reduce-scatter.7.cloned.1.call-start = ((), (), s32[]{:S(2)}) async-start(), calls=%async_computation.8 | async-start | bytes 4456448 | tf_op jit(solution)/shard_map/reduce_scatter | solution.py:126
  121.2 1.2 copy-start.6
  137.7 0.9 copy-start.25
  137.7 55.3 %copy-start.46 = (f32[128]{0:T(128)S(1)}, f32[128]{0:T(128)}, u32[]{:S(2)}) copy-start(f32[128]{0:T(128)} %param.14) | copy-start | bytes 1540
  137.7 57.1 %copy-start.26 = (f32[128,400]{0,1:T(8,128)S(1)}, f32[128,400]{0,1:T(8,128)}, u32[]{:S(2)}) copy-start(f32[128,400]{0,1:T(8,128)} %param.15) | copy-start | bytes 614404
  137.7 128.4 %copy-start.47 = (f32[128]{0:T(128)S(1)}, f32[128]{0:T(128)}, u32[]{:S(2)}) copy-start(f32[128]{0:T(128)} %param.16) | copy-start | bytes 1540
  137.7 139.1 %copy-start.33 = (s32[1024,1]{0,1:T(1,128)S(1)}, s32[1024,1]{0,1:T(1,128)}, u32[]{:S(2)}) copy-start(s32[1024,1]{0,1:T(1,128)} %get-tuple-element.30) | copy-start | bytes 12292
  137.7 139.1 %copy-start.44 = (s32[128,1]{0,1:T(1,128)S(1)}, s32[128,1]{0,1:T(1,128)}, u32[]{:S(2)}) copy-start(s32[128,1]{0,1:T(1,128)} %get-tuple-element.44) | copy-start | bytes 1540
  137.8 139.1 %copy-start.39 = (s32[128]{0:T(128)S(1)}, s32[128]{0:T(128)}, u32[]{:S(2)}) copy-start(s32[128]{0:T(128)} %get-tuple-element.46) | copy-start | bytes 1540
  137.8 164.4 %all-gather.9.cloned.1.call-start = ((), (), s32[]{:S(2)}) async-start(), calls=%async_computation.7 | async-start | bytes 2228224 | tf_op jit(solution)/shard_map/all_gather | solution.py:97
  138.8 138.2 %copy-start.21 = (f32[128,400]{1,0:T(8,128)}, f32[128,400]{1,0:T(8,128)S(1)}, u32[]{:S(2)}) copy-start(f32[128,400]{1,0:T(8,128)S(1)} %copy.45) | copy-start | bytes 614404
  194.8 146.1 %all-gather.11.cloned.1.call-start = ((), (), s32[]{:S(2)}) async-start(), calls=%async_computation.9 | async-start | bytes 2228224 | tf_op jit(solution)/shard_map/all_gather | solution.py:100
  267.2 8.0 %collective-permute-start = (f32[128,400]{1,0:T(8,128)S(1)}, f32[128,400]{1,0:T(8,128)S(1)}, u32[]{:S(2)}, u32[]{:S(2)}) collective-permute-start(f32[128,400]{1,0:T(8,128)S(1)} %divide_subtract_fusion.2), channel_id=1, source_target_pairs={{0,128},{16,144},{32,160},{48,176},{64,192},{80,208},{96,224},{112... | collective-permute-start | bytes 614408 | tf_op jit(solution)/shard_map/ppermute | solution.py:16
  275.2 0.7 copy-start.23
  276.6 192.1 %reduce-scatter.11.cloned.1.call-start = ((), (), s32[]{:S(2)}) async-start(), calls=%async_computation.11 | async-start | bytes 4456448 | tf_op jit(solution)/shard_map/reduce_scatter | solution.py:126
  277.0 31.5 %copy-start.35 = (pred[1024]{0:T(1024)(128)(4,1)S(1)}, pred[1024]{0:T(1024)(128)(4,1)}, u32[]{:S(2)}) copy-start(pred[1024]{0:T(1024)(128)(4,1)} %get-tuple-element.22) | copy-start | bytes 3076
  308.5 2.4 copy-start.12
  349.8 0.8 copy-start.43
  352.2 2.3 copy-start.7
  353.3 1.2 copy-start.3
  369.9 1.2 copy-start.8
  369.9 145.5 %reduce-scatter.9.cloned.1.call-start = ((), (), s32[]{:S(2)}) async-start(), calls=%async_computation.10 | async-start | bytes 4456448 | tf_op jit(solution)/shard_map/reduce_scatter | solution.py:120
  370.2 1.5 copy-start.4
  371.8 1.4 copy-start.2
  372.4 1.1 copy-start.18
  384.9 1.1 copy-start.11
  384.9 1.4 copy-start.15
  384.9 1.6 copy-start.17
  384.9 1.6 copy-start.32
  384.9 1.6 copy-start.38
  384.9 1.6 copy-start.41
  386.6 2.8 copy-start.13
  386.6 2.8 copy-start.19
  387.8 83.6 %copy-start.24 = (f32[128,400]{1,0:T(8,128)S(1)}, f32[128,400]{1,0:T(8,128)}, u32[]{:S(2)}) copy-start(f32[128,400]{1,0:T(8,128)} %copy-done.23) | copy-start | bytes 614404
  387.8 129.2 %copy-start.20 = (f32[128,400]{1,0:T(8,128)S(1)}, f32[128,400]{1,0:T(8,128)}, u32[]{:S(2)}) copy-start(f32[128,400]{1,0:T(8,128)} %reduce-scatter.5.cloned.1.call-done) | copy-start | bytes 614404
  387.8 129.2 %copy-start.22 = (f32[128,400]{1,0:T(8,128)S(1)}, f32[128,400]{1,0:T(8,128)}, u32[]{:S(2)}) copy-start(f32[128,400]{1,0:T(8,128)} %copy-done.21) | copy-start | bytes 614404
  387.8 82.0 %collective-permute-start.1 = (f32[128]{0:T(128)S(1)}, f32[128]{0:T(128)S(1)}, u32[]{:S(2)}, u32[]{:S(2)}) collective-permute-start(f32[128]{0:T(128)S(1)} %get-tuple-element.29), channel_id=1, source_target_pairs={{0,128},{16,144},{32,160},{48,176},{64,192},{80,208},{96,224},{112... | collective-permute-start | bytes 1544 | tf_op jit(solution)/shard_map/ppermute | solution.py:16
  389.4 130.9 %copy-start.1 = (f32[16,400]{1,0:T(8,128)S(1)}, f32[16,400]{1,0:T(8,128)}, u32[]{:S(2)}) copy-start(f32[16,400]{1,0:T(8,128)} %param.17) | copy-start | bytes 76804
  469.8 49.1 %collective-permute-start.3 = (f32[128]{0:T(128)S(1)}, f32[128]{0:T(128)S(1)}, u32[]{:S(2)}, u32[]{:S(2)}) collective-permute-start(f32[128]{0:T(128)S(1)} %get-tuple-element.25), channel_id=1, source_target_pairs={{0,128},{16,144},{32,160},{48,176},{64,192},{80,208},{96,224},{112... | collective-permute-start | bytes 1544 | tf_op jit(solution)/shard_map/ppermute | solution.py:16
  472.4 46.5 %collective-permute-start.2 = (f32[128,400]{1,0:T(8,128)S(1)}, f32[128,400]{1,0:T(8,128)S(1)}, u32[]{:S(2)}, u32[]{:S(2)}) collective-permute-start(f32[128,400]{1,0:T(8,128)S(1)} %divide_subtract_fusion), channel_id=1, source_target_pairs={{0,128},{16,144},{32,160},{48,176},{64,192},{80,208},{96,224},{112... | collective-permute-start | bytes 614408 | tf_op jit(solution)/shard_map/ppermute | solution.py:16
Sparse Core Ops, SparseCore 0:
  10.4 41.1 all-gather.6
  53.9 38.3 all-gather.4
  120.2 71.7 reduce-scatter.4
  194.4 70.6 reduce-scatter.6
  267.4 34.7 all-gather.8
  304.4 36.4 all-gather.10
  370.0 71.9 reduce-scatter.10
  444.6 70.7 reduce-scatter.8
where the time goes:
time: 537 us; the launch traced here: 527 us
  waiting for transfers between devices  292 us (54%)
  blocking collectives  77.5 us (14%)
  other arithmetic  64.7 us (12%)
  local copies, waits for them, and re-layouts  50.6 us (9%)
  matrix products  19.8 us (4%)
  between operations  15.3 us (3%)
  starting transfers between devices  7.14 us (1%)
    reduce_scatter x2, waiting for transfers between devices, per_device(): lax.psum_scatter(grad_term(grad_src, sources, rows_dev * lax.axis_size('r...  94 us
    psum x1, blocking collectives, per_device(): rel_total = rel_total + lax.psum(rel_term, ('dom', 'row'))  77.5 us
    reduce_scatter x2, waiting for transfers between devices, per_device(): lax.psum_scatter(grad_term(right_values, right_index, rows_dev * lax.axis...  70.1 us
    all_gather x2, waiting for transfers between devices, per_device(): lax.all_gather(right_low, 'row', axis=0, tiled=True)  63.9 us
    all_gather x2, waiting for transfers between devices, per_device(): lax.all_gather(left_low, 'row', axis=0, tiled=True)  57.5 us
    scatter-add x4, other arithmetic, grad_term(): jnp.zeros((row_count, values.shape[1]), jnp.float32).at[clipped].add(masked)  44.5 us
    gather x8, local copies, waits for them, and re-layouts, pick_rows(): rows = jnp.take(piece, jnp.clip(index, 0, row_count - 1), axis=0)  24.1 us
  transfers between devices with their start and end apart: 12, of which 8 were waited for; matrix products, arithmetic and copies ran while one was open for 13% of the time, Pallas kernels for 0%

commit v1 on v0

v1 whole, which is shorter than its diff:
```python
import functools

import jax
import jax.numpy as jnp
from jax import lax
from jax.experimental import pallas as pl
from jax.experimental.pallas import tpu as pltpu
from jax.sharding import PartitionSpec as P

ROUNDS = 2
STEP_SIZE = 0.1
EPSILON = 1e-10
MESH = pl.DeviceIdType.MESH
F32 = jnp.float32
BF16 = jnp.bfloat16
NT = (((1,), (1,)), ((), ()))
NN = (((1,), (0,)), ((), ()))
SEMS = 112


def dot(a, b, dims=NN):
    return lax.dot_general(a, b, dims, preferred_element_type=F32)


def split2(value):
    high = value.astype(BF16)
    return high, (value - high.astype(F32)).astype(BF16)


def window_kernel(
    dom_size, rel_scale,
    left_ref, left_state_ref, right_ref, right_state_ref, rel_ref, src_ref, relid_ref, dst_ref, neg_ref,
    left_out, left_state_out, right_out, right_state_out, rel_out,
    left_t, right_t, left_s, right_s, tab_l, tab_r, src_pos, right_pos,
    rel_rows, left_rows, anchor, right_rows, right_tr, weights, src_hl, right_hl,
    core_send, core_recv, x_send_r, x_recv_r, z_send_r, z_recv_r, own_r,
    x_send_l, x_recv_l, z_send_l, z_recv_l, y_send, y_recv,
    rel_part, rel_recv, send_sem, recv_sem,
):
    width, rows = left_t.shape
    edges = src_ref.shape[1]
    negs = neg_ref.shape[1]
    rels = rel_ref.shape[0]
    n_right = edges + negs
    neg_count = edges - 1 + negs
    dom = lax.axis_index("dom")
    row = lax.axis_index("row")
    x, z, c = row // 4, (row // 2) % 2, row % 2

    def row_peer(dx, dz, dc):
        return ((x + dx) % 4) * 4 + ((z + dz) % 2) * 2 + (c + dc) % 2

    core_peer = (dom, row_peer(0, 0, 1))
    z_peer = (dom, row_peer(0, 1, 0))
    x_peers = {dx: (dom, row_peer(dx, 0, 0)) for dx in (1, 2, 3)}
    y_peer = ((dom + dom_size // 2) % dom_size, row)
    if dom_size == 16:
        dom_groups = [
            {j: ((dom + 4 * j) % 16, row) for j in (1, 2, 3)},
            {j: ((dom // 4) * 4 + (dom % 4 + j) % 4, row) for j in (1, 2, 3)},
        ]
    else:
        dom_groups = [{2: y_peer}]
    peers = [core_peer, z_peer, *x_peers.values()]
    for group in dom_groups:
        peers += list(group.values())

    barrier = pltpu.get_barrier_semaphore()
    for peer in peers:
        pl.semaphore_signal(barrier, inc=1, device_id=peer, device_id_type=MESH)

    copies = []

    def send(src, dst, peer):
        k = len(copies)
        copy = pltpu.make_async_remote_copy(
            src_ref=src, dst_ref=dst, send_sem=send_sem.at[k], recv_sem=recv_sem.at[k],
            device_id=peer, device_id_type=MESH,
        )
        copy.start()
        copies.append(copy)
        return copy

    def place(cx, xx, zz):
        return cx * 8 + xx * 2 + zz

    mine = place(c, x, z)

    def positions(ids):
        return ((ids // 128) % 2) * 1024 + (ids // 256) * 128 + ids % 128

    def gather_left_start(rd):
        tab = tab_l.at[rd]
        own = tab.at[mine]
        zc = send(own, own, z_peer)
        xc = {dx: send(own, own, x_peers[dx]) for dx in (2, 1, 3)}
        return zc, xc

    def gather_right_start(rd):
        own = tab_r.at[rd, mine]
        xc = {dx: send(own, own, x_peers[dx]) for dx in (2, 1, 3)}
        zc = {0: send(own, own, z_peer)}
        return xc, zc

    def core_pair(tab, xx):
        part = tab.at[pl.ds(c * 8 + xx * 2, 2)]
        return send(part, part, core_peer)

    def gather_left_forward(rd, state):
        tab = tab_l.at[rd]
        zc, xc = state
        zc.wait_recv()
        other = tab.at[place(c, x, 1 - z)]
        xc2 = {dx: send(other, other, x_peers[dx]) for dx in (2, 1, 3)}
        return xc, xc2, [core_pair(tab, x)]

    def gather_left_core(rd, state):
        xc, xc2, cores = state
        for dx in (1, 3, 2):
            xc[dx].wait_recv()
            xc2[dx].wait_recv()
            cores.append(core_pair(tab_l.at[rd], (x + 4 - dx) % 4))
        return cores

    def gather_right_forward(rd, state):
        xc, zc = state
        tab = tab_r.at[rd]
        for dx in (1, 3, 2):
            xc[dx].wait_recv()
            got = tab.at[place(c, (x + 4 - dx) % 4, z)]
            zc[dx] = send(got, got, z_peer)
        return zc

    def gather_right_core(rd, zc):
        cores = []
        for dx in (0, 1, 3, 2):
            zc[dx].wait_recv()
            cores.append(core_pair(tab_r.at[rd], (x + 4 - dx) % 4))
        return cores

    def pick(tab, ids_ref, out_ref, tile_start, tile_len):
        table = jnp.concatenate([tab[p] for p in range(16)], axis=1)
        ids = ids_ref[:, pl.ds(tile_start, tile_len)]
        hot = lax.broadcasted_iota(jnp.int32, (16 * rows, tile_len), 0) == ids
        out_ref[:, pl.ds(tile_start, tile_len)] = dot(table, hot.astype(F32).astype(BF16)).astype(BF16)

    def scatter_unit(hl_ref, ids_ref, core, xx):
        sub = lax.broadcasted_iota(jnp.int32, (2 * rows, 1), 0)
        base = core * 8 * rows + xx * 2 * rows
        target = base + jnp.where(sub < rows, sub + (1 - z) * rows, sub - rows + z * rows)
        hot = (target == ids_ref[...]).astype(F32).astype(BF16)
        both = dot(hl_ref[...], hot, NT)
        return both[:width] + both[width:]

    def adagrad(rows_ref, state_ref, grad):
        state = state_ref[...] + jnp.sum(grad * grad, axis=0, keepdims=True) * (1.0 / width)
        state_ref[...] = state
        new = rows_ref[...] - grad * (STEP_SIZE / (jnp.sqrt(state) + EPSILON))
        rows_ref[...] = new
        return new

    left_t[...] = left_ref[...].T
    right_t[...] = right_ref[...].T
    tab_l[0, mine] = left_t[...].astype(BF16)
    tab_r[0, mine] = right_t[...].astype(BF16)
    left_s[...] = left_state_ref[...]
    right_s[...] = right_state_ref[...]
    pl.semaphore_wait(barrier, len(peers))

    left_state = gather_left_start(0)
    right_state = gather_right_start(0)

    rel_total = None
    for rd in range(ROUNDS):
        src_pos[...] = positions(src_ref[rd : rd + 1, :])
        right_pos[:, :edges] = positions(dst_ref[rd : rd + 1, :])
        right_pos[:, edges:] = positions(neg_ref[rd : rd + 1, :])
        rel_hot = (
            lax.broadcasted_iota(jnp.int32, (rels, edges), 0) == relid_ref[rd : rd + 1, :]
        ).astype(F32)
        rel_hot = rel_hot.astype(BF16)
        rel_value = rel_ref[...]
        high = rel_value.astype(BF16)
        rest = rel_value - high.astype(F32)
        mid = rest.astype(BF16)
        low = (rest - mid.astype(F32)).astype(BF16)
        rel_parts = jnp.concatenate([high.astype(F32).T, mid.astype(F32).T, low.astype(F32).T], axis=1)
        rel_rows[...] = dot(rel_parts.astype(BF16), jnp.concatenate([rel_hot] * 3, axis=0))

        left_state = gather_left_forward(rd, left_state)
        right_z = gather_right_forward(rd, right_state)
        left_cores = gather_left_core(rd, left_state)
        for copy in left_cores:
            copy.wait_recv()

        def pick_left(t, carry):
            pick(tab_l.at[rd], src_pos, left_rows, pl.multiple_of(t * 256, 256), 256)
            return carry

        lax.fori_loop(0, edges // 256, pick_left, 0)
        anchor[...] = (left_rows[...].astype(F32) * rel_rows[...]).astype(BF16)

        right_cores = gather_right_core(rd, right_z)
        for copy in right_cores:
            copy.wait_recv()

        def pick_right(t, carry):
            pick(tab_r.at[rd], right_pos, right_rows, pl.multiple_of(t * 256, 256), 256)
            return carry

        lax.fori_loop(0, edges // 256, pick_right, 0)
        pick(tab_r.at[rd], right_pos, right_rows, edges, negs)
        right_tr[...] = right_rows[...].astype(F32).T.astype(BF16)

        def score_block(b, carry):
            at = pl.multiple_of(b * 128, 128)
            scores = dot(right_tr[pl.ds(at, 128), :], anchor[...])
            weights[pl.ds(at, 128), :] = ((1.0 / (1.0 + jnp.exp(-scores))) * (1.0 / neg_count)).astype(BF16)
            return carry

        lax.fori_loop(0, n_right // 128, score_block, 0)

        def diag_block(b, carry):
            at = pl.multiple_of(b * 128, 128)
            scores = dot(right_tr[pl.ds(at, 128), :], anchor[:, pl.ds(at, 128)])
            eye = lax.broadcasted_iota(jnp.int32, (128, 128), 0) == lax.broadcasted_iota(jnp.int32, (128, 128), 1)
            own = -1.0 / (1.0 + jnp.exp(scores))
            rest = weights[pl.ds(at, 128), pl.ds(at, 128)].astype(F32)
            weights[pl.ds(at, 128), pl.ds(at, 128)] = jnp.where(eye, own, rest).astype(BF16)
            return carry

        lax.fori_loop(0, edges // 128, diag_block, 0)

        def grad_right(at, size):
            g = dot(anchor[...], weights[pl.ds(at, size), :], NT)
            high, low = split2(g)
            right_hl[:width, pl.ds(at, size)] = high
            right_hl[width:, pl.ds(at, size)] = low

        def grad_right_loop(t, carry):
            grad_right(pl.multiple_of(t * 256, 256), 256)
            return carry

        lax.fori_loop(0, edges // 256, grad_right_loop, 0)
        grad_right(edges, negs)

        order = (2, 1, 3, 0)

        def core_phase(hl_ref, ids_ref, base):
            sent = []
            for k, dx in enumerate(order):
                core_send[base + k] = scatter_unit(hl_ref, ids_ref, 1 - c, (x + dx) % 4)
                sent.append(send(core_send.at[base + k], core_recv.at[base + k], core_peer))
            return sent

        base = rd * 8
        sent = core_phase(right_hl, right_pos, base)
        z_copies = []
        for k, dx in enumerate(order):
            unit = scatter_unit(right_hl, right_pos, c, (x + dx) % 4)
            sent[k].wait_recv()
            unit = unit + core_recv[base + k]
            z_send_r[rd, k] = unit[:, :rows].astype(BF16)
            z_copies.append(send(z_send_r.at[rd, k], z_recv_r.at[rd, k], z_peer))
            own_r[k] = unit[:, rows:]

        def grad_left_loop(t, acc):
            at = pl.multiple_of(t * 256, 256)
            tile = pl.ds(at, 256)
            g = dot(right_rows[...], weights[:, tile])
            high, low = split2(g * rel_rows[:, tile])
            src_hl[:width, tile] = high
            src_hl[width:, tile] = low
            high, low = split2(g * left_rows[:, tile].astype(F32))
            hot = (
                lax.broadcasted_iota(jnp.int32, (128, 256), 0) == relid_ref[rd : rd + 1, tile]
            ).astype(F32)
            hot = hot.astype(BF16)
            return acc + dot(high, hot, NT) + dot(low, hot, NT)

        rel_acc = lax.fori_loop(0, edges // 256, grad_left_loop, jnp.zeros((width, 128), F32))
        rel_term = rel_acc.T[:rels]
        rel_total = rel_term if rel_total is None else rel_total + rel_term

        base = rd * 8 + 4
        sent = core_phase(src_hl, src_pos, base)
        x_copies = []
        own_l = None
        for k, dx in enumerate(order):
            unit = scatter_unit(src_hl, src_pos, c, (x + dx) % 4)
            sent[k].wait_recv()
            unit = unit + core_recv[base + k]
            if dx:
                x_send_l[rd, k] = unit.astype(BF16)
                x_copies.append(send(x_send_l.at[rd, k], x_recv_l.at[rd, k], x_peers[dx]))
            else:
                own_l = unit

        rel_stages = []
        if rd == ROUNDS - 1:
            rel_part[0] = rel_total
            rel_stages.append(send(rel_part.at[0], rel_recv.at[0], core_peer))

        right_x = []
        for k, dx in enumerate(order):
            z_copies[k].wait_recv()
            total = own_r[k] + z_recv_r[rd, k].astype(F32)
            if dx:
                x_send_r[rd, k] = total.astype(BF16)
                right_x.append(send(x_send_r.at[rd, k], x_recv_r.at[rd, k], x_peers[dx]))
            else:
                right_own = total
        own_r[3] = right_own

        def rel_step(slot, copies_in, last):
            values = {}
            for j, (copy, at) in copies_in.items():
                copy.wait_recv()
                values[j] = rel_recv[at]
            own = rel_part[slot]
            if len(values) == 3:
                total = (own + values[2]) + (values[1] + values[3])
            else:
                (only,) = values.values()
                total = own + only
            rel_part[slot + 1] = total
            return total

        if rd == ROUNDS - 1:
            rel_step(0, {0: (rel_stages[0], 0)}, False)
            rel_x = {j: (send(rel_part.at[1], rel_recv.at[j], x_peers[j]), j) for j in (1, 2, 3)}

        total = own_l
        for k in range(3):
            x_copies[k].wait_recv()
            total = total + x_recv_l[rd, k].astype(F32)
        z_send_l[rd] = total[:, :rows].astype(BF16)
        left_z = send(z_send_l.at[rd], z_recv_l.at[rd], z_peer)
        left_own = total[:, rows:]

        if rd == ROUNDS - 1:
            rel_step(1, rel_x, False)
            rel_z = {0: (send(rel_part.at[2], rel_recv.at[4], z_peer), 4)}

        total = own_r[3]
        for k in range(3):
            right_x[k].wait_recv()
            total = total + x_recv_r[rd, k].astype(F32)

        if rd < ROUNDS - 1:
            new = adagrad(right_t, right_s, total)
            y_send[...] = new.astype(BF16)
            to_holder = send(y_send, tab_r.at[rd + 1, mine], y_peer)
            left_z.wait_recv()
            new = adagrad(left_t, left_s, left_own + z_recv_l[rd].astype(F32))
            tab_l[rd + 1, mine] = new.astype(BF16)
            left_state = gather_left_start(rd + 1)
            to_holder.wait_recv()
            right_state = gather_right_start(rd + 1)
        else:
            own_r[0] = total
            to_owner = send(own_r.at[0], y_recv, y_peer)
            rel_step(2, rel_z, False)
            at = 5
            slot = 3
            rel_dom = {}
            for j, peer in dom_groups[0].items():
                rel_dom[j] = (send(rel_part.at[slot], rel_recv.at[at], peer), at)
                at += 1
            left_z.wait_recv()
            new = adagrad(left_t, left_s, left_own + z_recv_l[rd].astype(F32))
            left_out[...] = new.T
            left_state_out[...] = left_s[...]
            final = rel_step(slot, rel_dom, False)
            for group in dom_groups[1:]:
                slot += 1
                rel_dom = {}
                for j, peer in group.items():
                    rel_dom[j] = (send(rel_part.at[slot], rel_recv.at[at], peer), at)
                    at += 1
            to_owner.wait_recv()
            new = adagrad(right_t, right_s, y_recv[...])
            right_out[...] = new.T
            right_state_out[...] = right_s[...]
            if len(dom_groups) > 1:
                final = rel_step(slot, rel_dom, False)
            rel_out[...] = final * rel_scale

    for copy in copies:
        copy.wait_send()


def per_device(
    left_emb, left_state, right_emb, right_state, rel_diag, edge_src, edge_rel, edge_dst, neg_rows
):
    rows, width = left_emb.shape
    edges = edge_src.shape[1]
    negs = neg_rows.shape[2]
    rels = rel_diag.shape[0]
    n_right = edges + negs
    dom_size = lax.axis_size("dom")
    device_count = dom_size * lax.axis_size("row")
    rel_scale = (ROUNDS * edges * device_count) ** (-0.5)
    vmem = pltpu.VMEM
    outs = pl.pallas_call(
        functools.partial(window_kernel, dom_size, rel_scale),
        out_shape=(
            jax.ShapeDtypeStruct((rows, width), F32),
            jax.ShapeDtypeStruct((1, rows), F32),
            jax.ShapeDtypeStruct((rows, width), F32),
            jax.ShapeDtypeStruct((1, rows), F32),
            jax.ShapeDtypeStruct((rels, width), F32),
        ),
        in_specs=[pl.BlockSpec(memory_space=vmem)] * 9,
        out_specs=tuple([pl.BlockSpec(memory_space=vmem)] * 5),
        scratch_shapes=[
            vmem((width, rows), F32),
            vmem((width, rows), F32),
            vmem((1, rows), F32),
            vmem((1, rows), F32),
            vmem((ROUNDS, 16, width, rows), BF16),
            vmem((ROUNDS, 16, width, rows), BF16),
            vmem((1, edges), jnp.int32),
            vmem((1, n_right), jnp.int32),
            vmem((width, edges), F32),
            vmem((width, edges), BF16),
            vmem((width, edges), BF16),
            vmem((width, n_right), BF16),
            vmem((n_right, width), BF16),
            vmem((n_right, edges), BF16),
            vmem((2 * width, edges), BF16),
            vmem((2 * width, n_right), BF16),
            vmem((ROUNDS * 8, width, 2 * rows), F32),
            vmem((ROUNDS * 8, width, 2 * rows), F32),
            vmem((ROUNDS, 3, width, rows), BF16),
            vmem((ROUNDS, 3, width, rows), BF16),
            vmem((ROUNDS, 4, width, rows), BF16),
            vmem((ROUNDS, 4, width, rows), BF16),
            vmem((4, width, rows), F32),
            vmem((ROUNDS, 3, width, 2 * rows), BF16),
            vmem((ROUNDS, 3, width, 2 * rows), BF16),
            vmem((ROUNDS, width, rows), BF16),
            vmem((ROUNDS, width, rows), BF16),
            vmem((width, rows), BF16),
            vmem((width, rows), F32),
            vmem((6, rels, width), F32),
            vmem((11, rels, width), F32),
            pltpu.SemaphoreType.DMA((SEMS,)),
            pltpu.SemaphoreType.DMA((SEMS,)),
        ],
        compiler_params=pltpu.CompilerParams(
            collective_id=0, has_side_effects=True, vmem_limit_bytes=60 * 1024 * 1024
        ),
    )(
        left_emb, left_state[None], right_emb, right_state[None], rel_diag,
        edge_src, edge_rel, edge_dst, neg_rows.reshape(ROUNDS, negs),
    )
    left_new, left_sum, right_new, right_sum, rel = outs
    return left_new, left_sum.reshape(rows), right_new, right_sum.reshape(rows), rel


def solution(mesh):
    placed = (
        P(("dom", "row"), None),
        P(("dom", "row")),
        P(("dom", "row"), None),
        P(("dom", "row")),
        P(),
        P(None, ("dom", "row")),
        P(None, ("dom", "row")),
        P(None, ("dom", "row")),
        P(None, ("dom", "row"), None),
    )
    return jax.shard_map(
        per_device,
        mesh=mesh,
        in_specs=placed,
        out_specs=(
            P(("dom", "row"), None),
            P(("dom", "row")),
            P(("dom", "row"), None),
            P(("dom", "row")),
            P(),
        ),
        check_vma=False,
    )
```

time: 537 us -> 165 us (0.31); the launches traced: 527 us -> 165 us
  waiting for transfers between devices: 292 us -> 0 us
  Pallas kernels: 0 us -> 157 us
  blocking collectives: 77.5 us -> 0 us
  other arithmetic: 64.7 us -> 0 us
  local copies, waits for them, and re-layouts: 50.6 us -> 7.01 us
  matrix products: 19.8 us -> 0 us
  between operations: 15.3 us -> 0.66 us
  starting transfers between devices: 7.14 us -> 0 us
    reduce_scatter x4 -> x0, waiting for transfers between devices: 164 us -> none  [the longest x2 94 us: per_device(): lax.psum_scatter(grad_term(grad_src, sources, rows_dev * lax.axis_size('r...]
    pallas_call x0 -> x1, Pallas kernels: none -> 157 us  [per_device(): pl.pallas_call(functools.partial(window_kernel, dom_size, rel_scale), out...]
    all_gather x4 -> x0, waiting for transfers between devices: 121 us -> none  [the longest x2 63.9 us: per_device(): lax.all_gather(right_low, 'row', axis=0, tiled=True)]
    psum x1 -> x0, blocking collectives: 77.5 us -> none  [per_device(): rel_total = rel_total + lax.psum(rel_term, ('dom', 'row'))]
    scatter-add x4 -> x0, other arithmetic: 44.5 us -> none  [grad_term(): jnp.zeros((row_count, values.shape[1]), jnp.float32).at[clipped].add(masked)]
    gather x8 -> x0, local copies, waits for them, and re-layouts: 24.1 us -> none  [pick_rows(): rows = jnp.take(piece, jnp.clip(index, 0, row_count - 1), axis=0)]
    dot_general x28 -> x0, matrix products: 19.8 us -> none  [the longest x4 5.3 us: span_terms(): lax.dot_general(anchor_block, right_rows, (((1,), (1,)), ((), ())), prefe...]
    select_n x4 -> x0, local copies, waits for them, and re-layouts: 7.77 us -> none  [grad_term(): masked = jnp.where(inside[:, None], values, 0.0)]
  transfers between devices with their start and end apart: 12 -> 0, of which waited for: 8 -> 0; matrix products, arithmetic and copies ran while one was open for 13% -> 0% of each run, Pallas kernels for 0% -> 0%
where the time goes in v1:
time: 165 us
  Pallas kernels  157 us (95%)
  local copies, waits for them, and re-layouts  7.01 us (4%)
    pallas_call x1, Pallas kernels, per_device(): pl.pallas_call(functools.partial(window_kernel, dom_size, rel_scale), out...  157 us
    unnamed x17, local copies, waits for them, and re-layouts  7.01 us

profile of v1, /device:TPU:24, one launch (start us, length us, event | category | flops | bytes accessed | tf_op | source)
XLA Modules:
  0.0 164.6 jit_solution(11012569694009317162)
XLA Ops:
  0.6 0.0 copy-start.1
  0.6 1.8 %copy.14.left_ref = f32[128,400]{1,0:T(8,128)} copy(f32[128,400]{0,1:T(8,128)} %param.9) | data formatting | bytes 409600 | tf_op args[0]
  2.4 0.0 copy-done.1
  2.4 0.8 copy.15.right_ref
  3.3 157.0 %shard_map.128 = (f32[128,400]{1,0:T(8,128)}, f32[1,128]{1,0:T(1,128)}, f32[128,400]{1,0:T(8,128)}, f32[1,128]{1,0:T(1,128)}, f32[16,400]{1,0:T(8,128)}) custom-call(f32[128,400]{1,0:T(8,128)} %copy.14.left_ref, f32[1,128]{1,0:T(1,128)} %bitcast.6, f32[128,400]{1,0:T(8,128)} %copy.15.right_ref, f32[1,128]{1,0:T(1,128)} %bitcast.7, f32[16,400]{1,0:T(8,128)} %rel_ref.1, ...), custom_call_target="tpu_custom_call" | custom-call | tf_op jit(solution)/shard_map/pallas_call | solution.py:405
  160.2 0.0 copy-start
  160.3 1.8 %copy.16 = f32[128,400]{0,1:T(8,128)} copy(f32[128,400]{1,0:T(8,128)} %get-tuple-element.15) | data formatting | bytes 409600
  162.1 0.0 copy-done
  162.1 0.0 copy-start.4
  162.1 0.0 copy-start.2
  162.1 0.8 copy.17
  162.9 0.0 copy-done.4
  162.9 0.0 copy-start.3
  162.9 0.5 copy.21
  163.4 0.1 copy-done.3
  163.5 0.5 copy.22
  164.0 0.0 copy-done.2
  164.0 0.6 copy.23
Async XLA Ops:
  0.6 1.8 %copy-start.1 = (f32[128,400]{0,1:T(8,128)S(1)}, f32[128,400]{0,1:T(8,128)}, u32[]{:S(2)}) copy-start(f32[128,400]{0,1:T(8,128)} %param.11) | copy-start | bytes 614404
  160.2 1.8 %copy-start = (f32[128,400]{1,0:T(8,128)S(1)}, f32[128,400]{1,0:T(8,128)}, u32[]{:S(2)}) copy-start(f32[128,400]{1,0:T(8,128)} %get-tuple-element.17) | copy-start | bytes 614404
  162.1 0.8 copy-start.4
  162.1 2.0 %copy-start.2 = (f32[16,400]{1,0:T(8,128)S(1)}, f32[16,400]{1,0:T(8,128)}, u32[]{:S(2)}) copy-start(f32[16,400]{1,0:T(8,128)} %get-tuple-element.29) | copy-start | bytes 76804
  162.9 0.6 copy-start.3

commit v2 on v1

v2 whole, which is shorter than its diff:
```python
import functools

import jax
import jax.numpy as jnp
from jax import lax
from jax.experimental import pallas as pl
from jax.experimental.pallas import tpu as pltpu
from jax.sharding import PartitionSpec as P

ROUNDS = 2
STEP_SIZE = 0.1
EPSILON = 1e-10
MESH = pl.DeviceIdType.MESH
F32 = jnp.float32
BF16 = jnp.bfloat16
NT = (((1,), (1,)), ((), ()))
NN = (((1,), (0,)), ((), ()))
SEMS = 112


def dot(a, b, dims=NN):
    return lax.dot_general(a, b, dims, preferred_element_type=F32)


def stage(name, fn):
    with jax.named_scope(name):
        fn()


def split2(value):
    high = value.astype(BF16)
    return high, (value - high.astype(F32)).astype(BF16)


def window_kernel(
    dom_size, rel_scale,
    left_ref, left_state_ref, right_ref, right_state_ref, rel_ref, src_ref, relid_ref, dst_ref, neg_ref,
    left_out, left_state_out, right_out, right_state_out, rel_out,
    left_t, right_t, left_s, right_s, tab_l, tab_r, src_pos, right_pos,
    rel_rows, left_rows, anchor, right_rows, right_tr, weights, src_hl, right_hl,
    core_send, core_recv, x_send_r, x_recv_r, z_send_r, z_recv_r, own_r,
    x_send_l, x_recv_l, z_send_l, z_recv_l, own_l, unit_own, y_send, y_grad, y_recv,
    rel_part, rel_recv, send_sem, recv_sem,
):
    width, rows = left_t.shape
    edges = src_ref.shape[1]
    negs = neg_ref.shape[1]
    rels = rel_ref.shape[0]
    n_right = edges + negs
    neg_count = edges - 1 + negs
    dom = lax.axis_index("dom")
    row = lax.axis_index("row")
    x, z, c = row // 4, (row // 2) % 2, row % 2

    def row_peer(dx, dz, dc):
        return ((x + dx) % 4) * 4 + ((z + dz) % 2) * 2 + (c + dc) % 2

    core_peer = (dom, row_peer(0, 0, 1))
    z_peer = (dom, row_peer(0, 1, 0))
    x_peers = {dx: (dom, row_peer(dx, 0, 0)) for dx in (1, 2, 3)}
    y_peer = ((dom + dom_size // 2) % dom_size, row)
    if dom_size == 16:
        dom_groups = [
            {j: ((dom + 4 * j) % 16, row) for j in (1, 2, 3)},
            {j: ((dom // 4) * 4 + (dom % 4 + j) % 4, row) for j in (1, 2, 3)},
        ]
    else:
        dom_groups = [{2: y_peer}]
    peers = [core_peer, z_peer, *x_peers.values()]
    for group in dom_groups:
        peers += list(group.values())

    barrier = pltpu.get_barrier_semaphore()
    for peer in peers:
        pl.semaphore_signal(barrier, inc=1, device_id=peer, device_id_type=MESH)

    copies = []

    def send(src, dst, peer):
        k = len(copies)
        copy = pltpu.make_async_remote_copy(
            src_ref=src, dst_ref=dst, send_sem=send_sem.at[k], recv_sem=recv_sem.at[k],
            device_id=peer, device_id_type=MESH,
        )
        copy.start()
        copies.append(copy)
        return copy

    def place(cx, xx, zz):
        return cx * 8 + xx * 2 + zz

    mine = place(c, x, z)

    def positions(ids):
        return ((ids // 128) % 2) * 1024 + (ids // 256) * 128 + ids % 128

    def gather_left_start(rd):
        own = tab_l.at[rd, mine]
        zc = send(own, own, z_peer)
        return zc, {dx: send(own, own, x_peers[dx]) for dx in (2, 1, 3)}

    def gather_right_start(rd):
        own = tab_r.at[rd, mine]
        xc = {dx: send(own, own, x_peers[dx]) for dx in (2, 1, 3)}
        return xc, {0: send(own, own, z_peer)}

    def core_pair(tab, xx):
        part = tab.at[pl.ds(c * 8 + xx * 2, 2)]
        return send(part, part, core_peer)

    def pick_half(tab, ids_ref, out_ref, core, first):
        def tile(start, size):
            ids = ids_ref[:, pl.ds(start, size)] - core * 8 * rows
            hot = (lax.broadcasted_iota(jnp.int32, (8 * rows, size), 0) == ids).astype(F32).astype(BF16)
            table = jnp.concatenate([tab[core * 8 + p] for p in range(8)], axis=1)
            got = dot(table, hot).astype(BF16)
            if not first:
                got = got + out_ref[:, pl.ds(start, size)]
            out_ref[:, pl.ds(start, size)] = got

        def body(t, carry):
            tile(pl.multiple_of(t * 256, 256), 256)
            return carry

        count = ids_ref.shape[1]
        lax.fori_loop(0, count // 256, body, 0)
        if count % 256:
            tile(count - count % 256, count % 256)

    def pick_left(rd, core, first=False):
        stage("pick_left", lambda: pick_half(tab_l.at[rd], src_pos, left_rows, core, first))

    def pick_right(rd, core, first=False):
        stage("pick_right", lambda: pick_half(tab_r.at[rd], right_pos, right_rows, core, first))

    def scatter_unit(hl_ref, ids_ref, core, xx):
        sub = lax.broadcasted_iota(jnp.int32, (2 * rows, 1), 0)
        base = core * 8 * rows + xx * 2 * rows
        target = base + jnp.where(sub < rows, sub + (1 - z) * rows, sub - rows + z * rows)
        hot = (target == ids_ref[...]).astype(F32).astype(BF16)
        both = dot(hl_ref[...], hot, NT)
        return both[:width] + both[width:]

    def adagrad(rows_ref, state_ref, grad):
        state = state_ref[...] + jnp.sum(grad * grad, axis=0, keepdims=True) * (1.0 / width)
        state_ref[...] = state
        new = rows_ref[...] - grad * (STEP_SIZE / (jnp.sqrt(state) + EPSILON))
        rows_ref[...] = new
        return new

    def load():
        left_t[...] = left_ref[...].T
        right_t[...] = right_ref[...].T
        tab_l[0, mine] = left_t[...].astype(BF16)
        tab_r[0, mine] = right_t[...].astype(BF16)
        left_s[...] = left_state_ref[...]
        right_s[...] = right_state_ref[...]

    stage("load_transpose", load)
    pl.semaphore_wait(barrier, len(peers))

    right_state = gather_right_start(0)
    left_state = gather_left_start(0)

    rel_total = None
    for rd in range(ROUNDS):
        def indices():
            src_pos[...] = positions(src_ref[rd : rd + 1, :])
            right_pos[:, :edges] = positions(dst_ref[rd : rd + 1, :])
            right_pos[:, edges:] = positions(neg_ref[rd : rd + 1, :])
            rel_hot = (
                lax.broadcasted_iota(jnp.int32, (rels, edges), 0) == relid_ref[rd : rd + 1, :]
            ).astype(F32)
            rel_hot = rel_hot.astype(BF16)
            rel_value = rel_ref[...]
            high = rel_value.astype(BF16)
            rest = rel_value - high.astype(F32)
            mid = rest.astype(BF16)
            low = (rest - mid.astype(F32)).astype(BF16)
            rel_parts = jnp.concatenate([high.astype(F32).T, mid.astype(F32).T, low.astype(F32).T], axis=1)
            rel_rows[...] = dot(rel_parts.astype(BF16), jnp.concatenate([rel_hot] * 3, axis=0))

        stage("indices_relation", indices)

        right_x, right_z = right_state
        left_z, left_x = left_state
        left_cores, right_cores = {}, {}
        left_z.wait_recv()
        got = tab_l.at[rd, place(c, x, 1 - z)]
        left_x2 = {dx: send(got, got, x_peers[dx]) for dx in (2, 1, 3)}
        left_cores[0] = core_pair(tab_l.at[rd], x)
        for dx in (1, 3, 2):
            right_x[dx].wait_recv()
            got = tab_r.at[rd, place(c, (x + 4 - dx) % 4, z)]
            right_z[dx] = send(got, got, z_peer)
        for dx in (0, 1, 3, 2):
            from_x = (x + 4 - dx) % 4
            right_z[dx].wait_recv()
            right_cores[dx] = core_pair(tab_r.at[rd], from_x)
            if dx:
                left_x[dx].wait_recv()
                left_x2[dx].wait_recv()
                left_cores[dx] = core_pair(tab_l.at[rd], from_x)
        pick_left(rd, c, True)
        pick_right(rd, c, True)
        for dx in (0, 1, 3, 2):
            left_cores[dx].wait_recv()
        pick_left(rd, 1 - c)
        for dx in (0, 1, 3, 2):
            right_cores[dx].wait_recv()
        pick_right(rd, 1 - c)

        def transposes():
            anchor[...] = (left_rows[...].astype(F32) * rel_rows[...]).astype(BF16)
            right_tr[...] = right_rows[...].astype(F32).T.astype(BF16)

        stage("anchor_transpose", transposes)

        def score_tile(t, carry):
            tile = pl.ds(pl.multiple_of(t * 256, 256), 256)
            scores = dot(right_tr[...], anchor[:, tile])
            weights[:, tile] = ((1.0 / (1.0 + jnp.exp(-scores))) * (1.0 / neg_count)).astype(BF16)
            scores = dot(right_tr[tile, :], anchor[:, tile])
            eye = lax.broadcasted_iota(jnp.int32, (256, 256), 0) == lax.broadcasted_iota(jnp.int32, (256, 256), 1)
            own = -1.0 / (1.0 + jnp.exp(scores))
            rest = weights[tile, tile].astype(F32)
            weights[tile, tile] = jnp.where(eye, own, rest).astype(BF16)
            return carry

        stage("scores", lambda: lax.fori_loop(0, edges // 256, score_tile, 0))

        def grad_right(at, size):
            g = dot(anchor[...], weights[pl.ds(at, size), :], NT)
            high, low = split2(g)
            right_hl[:width, pl.ds(at, size)] = high
            right_hl[width:, pl.ds(at, size)] = low

        def grad_right_loop(t, carry):
            grad_right(pl.multiple_of(t * 256, 256), 256)
            return carry

        def grad_right_all():
            lax.fori_loop(0, edges // 256, grad_right_loop, 0)
            grad_right(edges, negs)

        stage("grad_right", grad_right_all)

        order = (2, 1, 3, 0)

        def scatter(name, hl_ref, ids_ref, base, use):
            sent = {}

            def partner(k):
                def part():
                    core_send[base + k] = scatter_unit(hl_ref, ids_ref, 1 - c, (x + order[k]) % 4)

                stage(name, part)
                sent[k] = send(core_send.at[base + k], core_recv.at[base + k], core_peer)

            def own(k):
                def part():
                    unit_own[...] = scatter_unit(hl_ref, ids_ref, c, (x + order[k]) % 4)

                stage(name, part)
                sent[k].wait_recv()
                use(k, unit_own[...] + core_recv[base + k])

            partner(0)
            partner(1)
            own(0)
            partner(2)
            own(1)
            partner(3)
            own(2)
            own(3)

        right_x = {}

        def use_right(k, unit):
            if order[k]:
                x_send_r[rd, k] = unit.astype(BF16)
                right_x[k] = send(x_send_r.at[rd, k], x_recv_r.at[rd, k], x_peers[order[k]])
            else:
                own_r[...] = unit

        scatter("scatter_right", right_hl, right_pos, rd * 8, use_right)

        def grad_left_loop(t, acc):
            at = pl.multiple_of(t * 256, 256)
            tile = pl.ds(at, 256)
            g = dot(right_rows[...], weights[:, tile])
            high, low = split2(g * rel_rows[:, tile])
            src_hl[:width, tile] = high
            src_hl[width:, tile] = low
            high, low = split2(g * left_rows[:, tile].astype(F32))
            hot = (
                lax.broadcasted_iota(jnp.int32, (128, 256), 0) == relid_ref[rd : rd + 1, tile]
            ).astype(F32)
            hot = hot.astype(BF16)
            return acc + dot(high, hot, NT) + dot(low, hot, NT)

        def grad_left_all():
            rel_acc = lax.fori_loop(0, edges // 256, grad_left_loop, jnp.zeros((width, 128), F32))
            rel_part[5] = rel_acc.T[:rels]

        stage("grad_left", grad_left_all)
        rel_term = rel_part[5]
        rel_total = rel_term if rel_total is None else rel_total + rel_term
        last = rd == ROUNDS - 1
        rel_wait = None

        def rel_start(slot, at, group):
            return {j: (send(rel_part.at[slot], rel_recv.at[at + n], group[j]), at + n) for n, j in enumerate(group)}

        def rel_step(slot, arriving):
            values = {}
            for j, (copy, at) in arriving.items():
                copy.wait_recv()
                values[j] = rel_recv[at]
            own = rel_part[slot]
            if len(values) == 3:
                total = (own + values[2]) + (values[1] + values[3])
            else:
                (only,) = values.values()
                total = own + only
            rel_part[slot + 1] = total

        if last:
            rel_part[0] = rel_total
            rel_wait = rel_start(0, 0, {1: core_peer})

        left_z = {}

        def use_left(k, unit):
            z_send_l[rd, k] = unit[:, :rows].astype(BF16)
            left_z[k] = send(z_send_l.at[rd, k], z_recv_l.at[rd, k], z_peer)
            own_l[k] = unit[:, rows:]

        scatter("scatter_left", src_hl, src_pos, rd * 8 + 4, use_left)

        if last:
            rel_step(0, rel_wait)
            rel_wait = rel_start(1, 1, x_peers)

        total = own_r[...]
        for k in range(3):
            right_x[k].wait_recv()
            total = total + x_recv_r[rd, k].astype(F32)
        z_send_r[rd] = total[:, :rows].astype(BF16)
        right_z = send(z_send_r.at[rd], z_recv_r.at[rd], z_peer)
        own_r[:, rows:] = total[:, rows:]

        left_x = {}

        def left_on(k):
            left_z[k].wait_recv()
            total = own_l[k] + z_recv_l[rd, k].astype(F32)
            if order[k]:
                x_send_l[rd, k] = total.astype(BF16)
                left_x[k] = send(x_send_l.at[rd, k], x_recv_l.at[rd, k], x_peers[order[k]])
            else:
                own_l[k] = total

        left_on(0)
        left_on(1)
        if last:
            rel_step(1, rel_wait)
            rel_wait = rel_start(2, 4, {1: z_peer})

        right_z.wait_recv()
        total = own_r[:, rows:] + z_recv_r[rd].astype(F32)
        if last:
            y_grad[...] = total
            to_owner = send(y_grad, y_recv, y_peer)
        else:
            new = adagrad(right_t, right_s, total)
            y_send[...] = new.astype(BF16)
            to_holder = send(y_send, tab_r.at[rd + 1, mine], y_peer)
        left_on(2)
        if last:
            rel_step(2, rel_wait)
            rel_wait = rel_start(3, 5, dom_groups[0])
        left_on(3)
        if not last:
            to_holder.wait_recv()
            right_state = gather_right_start(rd + 1)
        total = own_l[3]
        for k in range(3):
            left_x[k].wait_recv()
            total = total + x_recv_l[rd, k].astype(F32)
        new = adagrad(left_t, left_s, total)
        if not last:
            tab_l[rd + 1, mine] = new.astype(BF16)
            left_state = gather_left_start(rd + 1)
        else:
            rel_step(3, rel_wait)
            if len(dom_groups) > 1:
                rel_wait = rel_start(4, 8, dom_groups[1])
            left_out[...] = new.T
            left_state_out[...] = left_s[...]
            to_owner.wait_recv()
            new = adagrad(right_t, right_s, y_recv[...])
            right_out[...] = new.T
            right_state_out[...] = right_s[...]
            if len(dom_groups) > 1:
                rel_step(4, rel_wait)
            rel_out[...] = rel_part[3 + len(dom_groups)] * rel_scale

    for copy in copies:
        copy.wait_send()


def per_device(
    left_emb, left_state, right_emb, right_state, rel_diag, edge_src, edge_rel, edge_dst, neg_rows
):
    rows, width = left_emb.shape
    edges = edge_src.shape[1]
    negs = neg_rows.shape[2]
    rels = rel_diag.shape[0]
    n_right = edges + negs
    dom_size = lax.axis_size("dom")
    device_count = dom_size * lax.axis_size("row")
    rel_scale = (ROUNDS * edges * device_count) ** (-0.5)
    vmem = pltpu.VMEM
    outs = pl.pallas_call(
        functools.partial(window_kernel, dom_size, rel_scale),
        out_shape=(
            jax.ShapeDtypeStruct((rows, width), F32),
            jax.ShapeDtypeStruct((1, rows), F32),
            jax.ShapeDtypeStruct((rows, width), F32),
            jax.ShapeDtypeStruct((1, rows), F32),
            jax.ShapeDtypeStruct((rels, width), F32),
        ),
        in_specs=[pl.BlockSpec(memory_space=vmem)] * 9,
        out_specs=tuple([pl.BlockSpec(memory_space=vmem)] * 5),
        scratch_shapes=[
            vmem((width, rows), F32),
            vmem((width, rows), F32),
            vmem((1, rows), F32),
            vmem((1, rows), F32),
            vmem((ROUNDS, 16, width, rows), BF16),
            vmem((ROUNDS, 16, width, rows), BF16),
            vmem((1, edges), jnp.int32),
            vmem((1, n_right), jnp.int32),
            vmem((width, edges), F32),
            vmem((width, edges), BF16),
            vmem((width, edges), BF16),
            vmem((width, n_right), BF16),
            vmem((n_right, width), BF16),
            vmem((n_right, edges), BF16),
            vmem((2 * width, edges), BF16),
            vmem((2 * width, n_right), BF16),
            vmem((ROUNDS * 8, width, 2 * rows), F32),
            vmem((ROUNDS * 8, width, 2 * rows), F32),
            vmem((ROUNDS, 3, width, 2 * rows), BF16),
            vmem((ROUNDS, 3, width, 2 * rows), BF16),
            vmem((ROUNDS, width, rows), BF16),
            vmem((ROUNDS, width, rows), BF16),
            vmem((width, 2 * rows), F32),
            vmem((ROUNDS, 3, width, rows), BF16),
            vmem((ROUNDS, 3, width, rows), BF16),
            vmem((ROUNDS, 4, width, rows), BF16),
            vmem((ROUNDS, 4, width, rows), BF16),
            vmem((4, width, rows), F32),
            vmem((width, 2 * rows), F32),
            vmem((width, rows), BF16),
            vmem((width, rows), F32),
            vmem((width, rows), F32),
            vmem((6, rels, width), F32),
            vmem((11, rels, width), F32),
            pltpu.SemaphoreType.DMA((SEMS,)),
            pltpu.SemaphoreType.DMA((SEMS,)),
        ],
        compiler_params=pltpu.CompilerParams(
            collective_id=0, has_side_effects=True, vmem_limit_bytes=60 * 1024 * 1024
        ),
    )(
        left_emb, left_state[None], right_emb, right_state[None], rel_diag,
        edge_src, edge_rel, edge_dst, neg_rows.reshape(ROUNDS, negs),
    )
    left_new, left_sum, right_new, right_sum, rel = outs
    return left_new, left_sum.reshape(rows), right_new, right_sum.reshape(rows), rel


def solution(mesh):
    placed = (
        P(("dom", "row"), None),
        P(("dom", "row")),
        P(("dom", "row"), None),
        P(("dom", "row")),
        P(),
        P(None, ("dom", "row")),
        P(None, ("dom", "row")),
        P(None, ("dom", "row")),
        P(None, ("dom", "row"), None),
    )
    return jax.shard_map(
        per_device,
        mesh=mesh,
        in_specs=placed,
        out_specs=(
            P(("dom", "row"), None),
            P(("dom", "row")),
            P(("dom", "row"), None),
            P(("dom", "row")),
            P(),
        ),
        check_vma=False,
    )
```

time: 165 us -> 149 us (0.903)
  Pallas kernels: 157 us -> 141 us
    pallas_call x1, Pallas kernels: 157 us -> 141 us  [per_device(): pl.pallas_call(functools.partial(window_kernel, dom_size, rel_scale), out...]
where the time goes in v2:
time: 149 us
  Pallas kernels  141 us (95%)
  local copies, waits for them, and re-layouts  7.01 us (5%)
    pallas_call x1, Pallas kernels, per_device(): pl.pallas_call(functools.partial(window_kernel, dom_size, rel_scale), out...  141 us
    unnamed x17, local copies, waits for them, and re-layouts  7.01 us

profile of v2, /device:TPU:24, one launch (start us, length us, event | category | flops | bytes accessed | tf_op | source)
XLA Modules:
  0.0 148.8 jit_solution(8020226636103738095)
XLA Ops:
  0.6 0.0 copy-start.1
  0.6 1.8 %copy.14.left_ref = f32[128,400]{1,0:T(8,128)} copy(f32[128,400]{0,1:T(8,128)} %param.9) | data formatting | bytes 409600 | tf_op args[0]
  2.4 0.0 copy-done.1
  2.4 0.8 copy.15.right_ref
  3.3 141.1 %shard_map.128 = (f32[128,400]{1,0:T(8,128)}, f32[1,128]{1,0:T(1,128)}, f32[128,400]{1,0:T(8,128)}, f32[1,128]{1,0:T(1,128)}, f32[16,400]{1,0:T(8,128)}) custom-call(f32[128,400]{1,0:T(8,128)} %copy.14.left_ref, f32[1,128]{1,0:T(1,128)} %bitcast.6, f32[128,400]{1,0:T(8,128)} %copy.15.right_ref, f32[1,128]{1,0:T(1,128)} %bitcast.7, f32[16,400]{1,0:T(8,128)} %rel_ref.1, ...), custom_call_target="tpu_custom_call" | custom-call | tf_op jit(solution)/shard_map/pallas_call | solution.py:425
  144.4 0.0 copy-start
  144.4 1.8 %copy.16 = f32[128,400]{0,1:T(8,128)} copy(f32[128,400]{1,0:T(8,128)} %get-tuple-element.15) | data formatting | bytes 409600
  146.2 0.0 copy-done
  146.2 0.0 copy-start.4
  146.2 0.0 copy-start.2
  146.2 0.8 copy.17
  147.1 0.0 copy-done.4
  147.1 0.0 copy-start.3
  147.1 0.5 copy.21
  147.6 0.1 copy-done.3
  147.7 0.5 copy.22
  148.2 0.0 copy-done.2
  148.2 0.6 copy.23
Async XLA Ops:
  0.6 1.8 %copy-start.1 = (f32[128,400]{0,1:T(8,128)S(1)}, f32[128,400]{0,1:T(8,128)}, u32[]{:S(2)}) copy-start(f32[128,400]{0,1:T(8,128)} %param.11) | copy-start | bytes 614404
  144.4 1.8 %copy-start = (f32[128,400]{1,0:T(8,128)S(1)}, f32[128,400]{1,0:T(8,128)}, u32[]{:S(2)}) copy-start(f32[128,400]{1,0:T(8,128)} %get-tuple-element.17) | copy-start | bytes 614404
  146.2 0.8 copy-start.4
  146.2 2.0 %copy-start.2 = (f32[16,400]{1,0:T(8,128)S(1)}, f32[16,400]{1,0:T(8,128)}, u32[]{:S(2)}) copy-start(f32[16,400]{1,0:T(8,128)} %get-tuple-element.29) | copy-start | bytes 76804
  147.1 0.6 copy-start.3

commit v3 on v2

--- a/solution.py
+++ b/solution.py
@@ -15,7 +15,7 @@
 BF16 = jnp.bfloat16
 NT = (((1,), (1,)), ((), ()))
 NN = (((1,), (0,)), ((), ()))
-SEMS = 112
+SEMS = 128
 
 
 def dot(a, b, dims=NN):
@@ -38,11 +38,12 @@
     left_out, left_state_out, right_out, right_state_out, rel_out,
     left_t, right_t, left_s, right_s, tab_l, tab_r, src_pos, right_pos,
     rel_rows, left_rows, anchor, right_rows, right_tr, weights, src_hl, right_hl,
-    core_send, core_recv, x_send_r, x_recv_r, z_send_r, z_recv_r, own_r,
-    x_send_l, x_recv_l, z_send_l, z_recv_l, own_l, unit_own, y_send, y_grad, y_recv,
+    core_send, core_recv, unit_own,
+    xa_send, xa_recv, za_send, za_recv, own_a, zb_send, zb_recv, xb_send, xb_recv, own_b, y_send, y_grad, y_recv,
     rel_part, rel_recv, send_sem, recv_sem,
 ):
     width, rows = left_t.shape
+    top = width // 2 // 16 * 16
     edges = src_ref.shape[1]
     negs = neg_ref.shape[1]
     rels = rel_ref.shape[0]
@@ -149,8 +150,8 @@
         return new
 
     def load():
-        left_t[...] = left_ref[...].T
-        right_t[...] = right_ref[...].T
+        left_t[...] = left_ref[...]
+        right_t[...] = right_ref[...]
         tab_l[0, mine] = left_t[...].astype(BF16)
         tab_r[0, mine] = right_t[...].astype(BF16)
         left_s[...] = left_state_ref[...]
@@ -194,27 +195,30 @@
             got = tab_r.at[rd, place(c, (x + 4 - dx) % 4, z)]
             right_z[dx] = send(got, got, z_peer)
         for dx in (0, 1, 3, 2):
-            from_x = (x + 4 - dx) % 4
             right_z[dx].wait_recv()
-            right_cores[dx] = core_pair(tab_r.at[rd], from_x)
-            if dx:
-                left_x[dx].wait_recv()
-                left_x2[dx].wait_recv()
-                left_cores[dx] = core_pair(tab_l.at[rd], from_x)
+            right_cores[dx] = core_pair(tab_r.at[rd], (x + 4 - dx) % 4)
+        pick_right(rd, c, True)
+        for dx in (1, 3, 2):
+            left_x[dx].wait_recv()
+            left_x2[dx].wait_recv()
+            left_cores[dx] = core_pair(tab_l.at[rd], (x + 4 - dx) % 4)
+        for dx in (0, 1, 3, 2):
+            right_cores[dx].wait_recv()
+        pick_right(rd, 1 - c)
+
+        def transpose():
+            right_tr[...] = right_rows[...].astype(F32).T.astype(BF16)
+
+        stage("transpose", transpose)
         pick_left(rd, c, True)
-        pick_right(rd, c, True)
         for dx in (0, 1, 3, 2):
             left_cores[dx].wait_recv()
         pick_left(rd, 1 - c)
-        for dx in (0, 1, 3, 2):
-            right_cores[dx].wait_recv()
-        pick_right(rd, 1 - c)
-
-        def transposes():
+
+        def anchors():
             anchor[...] = (left_rows[...].astype(F32) * rel_rows[...]).astype(BF16)
-            right_tr[...] = right_rows[...].astype(F32).T.astype(BF16)
-
-        stage("anchor_transpose", transposes)
+
+        stage("anchor", anchors)
 
         def score_tile(t, carry):
             tile = pl.ds(pl.multiple_of(t * 256, 256), 256)
@@ -247,7 +251,7 @@
 
         order = (2, 1, 3, 0)
 
-        def scatter(name, hl_ref, ids_ref, base, use):
+        def scatter(name, hl_ref, ids_ref, base, use, between=lambda k: None):
             sent = {}
 
             def partner(k):
@@ -264,6 +268,7 @@
                 stage(name, part)
                 sent[k].wait_recv()
                 use(k, unit_own[...] + core_recv[base + k])
+                between(k)
 
             partner(0)
             partner(1)
@@ -274,16 +279,52 @@
             own(2)
             own(3)
 
-        right_x = {}
-
-        def use_right(k, unit):
-            if order[k]:
-                x_send_r[rd, k] = unit.astype(BF16)
-                right_x[k] = send(x_send_r.at[rd, k], x_recv_r.at[rd, k], x_peers[order[k]])
-            else:
-                own_r[...] = unit
-
-        scatter("scatter_right", right_hl, right_pos, rd * 8, use_right)
+        def sums(side):
+            at = rd * 2 + side
+            az, ax, bx = {}, {}, {}
+            part = {}
+
+            def use(k, unit):
+                if order[k]:
+                    xa_send[at, k] = unit[:top].astype(BF16)
+                    ax[k] = send(xa_send.at[at, k], xa_recv.at[at, k], x_peers[order[k]])
+                else:
+                    own_a[side] = unit[:top]
+                zb_send[at, k] = unit[top:, :rows].astype(BF16)
+                az[k] = send(zb_send.at[at, k], zb_recv.at[at, k], z_peer)
+                own_b[side * 4 + k] = unit[top:, rows:]
+
+            def rest_on(k):
+                az[k].wait_recv()
+                total = own_b[side * 4 + k] + zb_recv[at, k].astype(F32)
+                if order[k]:
+                    xb_send[at, k] = total.astype(BF16)
+                    bx[k] = send(xb_send.at[at, k], xb_recv.at[at, k], x_peers[order[k]])
+                else:
+                    own_b[side * 4 + k] = total
+
+            def top_on():
+                total = own_a[side]
+                for k in range(3):
+                    ax[k].wait_recv()
+                    total = total + xa_recv[at, k].astype(F32)
+                za_send[at] = total[:, :rows].astype(BF16)
+                part["z"] = send(za_send.at[at], za_recv.at[at], z_peer)
+                own_a[side, :, rows:] = total[:, rows:]
+
+            def finish():
+                total = own_b[side * 4 + 3]
+                for k in range(3):
+                    bx[k].wait_recv()
+                    total = total + xb_recv[at, k].astype(F32)
+                part["z"].wait_recv()
+                return jnp.concatenate([own_a[side, :, rows:] + za_recv[at].astype(F32), total], axis=0)
+
+            return use, rest_on, top_on, finish
+
+        right_use, right_on, right_top, right_finish = sums(0)
+        left_use, left_on, left_top, left_finish = sums(1)
+        scatter("scatter_right", right_hl, right_pos, rd * 8, right_use)
 
         def grad_left_loop(t, acc):
             at = pl.multiple_of(t * 256, 256)
@@ -329,78 +370,57 @@
             rel_part[0] = rel_total
             rel_wait = rel_start(0, 0, {1: core_peer})
 
-        left_z = {}
-
-        def use_left(k, unit):
-            z_send_l[rd, k] = unit[:, :rows].astype(BF16)
-            left_z[k] = send(z_send_l.at[rd, k], z_recv_l.at[rd, k], z_peer)
-            own_l[k] = unit[:, rows:]
-
-        scatter("scatter_left", src_hl, src_pos, rd * 8 + 4, use_left)
-
-        if last:
-            rel_step(0, rel_wait)
-            rel_wait = rel_start(1, 1, x_peers)
-
-        total = own_r[...]
-        for k in range(3):
-            right_x[k].wait_recv()
-            total = total + x_recv_r[rd, k].astype(F32)
-        z_send_r[rd] = total[:, :rows].astype(BF16)
-        right_z = send(z_send_r.at[rd], z_recv_r.at[rd], z_peer)
-        own_r[:, rows:] = total[:, rows:]
-
-        left_x = {}
-
-        def left_on(k):
-            left_z[k].wait_recv()
-            total = own_l[k] + z_recv_l[rd, k].astype(F32)
-            if order[k]:
-                x_send_l[rd, k] = total.astype(BF16)
-                left_x[k] = send(x_send_l.at[rd, k], x_recv_l.at[rd, k], x_peers[order[k]])
-            else:
-                own_l[k] = total
-
-        left_on(0)
-        left_on(1)
+        right_on(0)
+        right_on(1)
+
+        def between(k):
+            nonlocal rel_wait
+            if k == 0:
+                right_on(2)
+                right_on(3)
+                if last:
+                    rel_step(0, rel_wait)
+                    rel_wait = rel_start(1, 1, x_peers)
+            if k == 1:
+                right_top()
+
+        scatter("scatter_left", src_hl, src_pos, rd * 8 + 4, left_use, between)
+
         if last:
             rel_step(1, rel_wait)
             rel_wait = rel_start(2, 4, {1: z_peer})
-
-        right_z.wait_recv()
-        total = own_r[:, rows:] + z_recv_r[rd].astype(F32)
+        left_on(0)
+        left_on(1)
+        total = right_finish()
         if last:
             y_grad[...] = total
             to_owner = send(y_grad, y_recv, y_peer)
+            rel_step(2, rel_wait)
+            rel_wait = rel_start(3, 5, dom_groups[0])
         else:
             new = adagrad(right_t, right_s, total)
             y_send[...] = new.astype(BF16)
             to_holder = send(y_send, tab_r.at[rd + 1, mine], y_peer)
         left_on(2)
+        left_on(3)
+        left_top()
         if last:
-            rel_step(2, rel_wait)
-            rel_wait = rel_start(3, 5, dom_groups[0])
-        left_on(3)
-        if not last:
+            rel_step(3, rel_wait)
+            if len(dom_groups) > 1:
+                rel_wait = rel_start(4, 8, dom_groups[1])
+        else:
             to_holder.wait_recv()
             right_state = gather_right_start(rd + 1)
-        total = own_l[3]
-        for k in range(3):
-            left_x[k].wait_recv()
-            total = total + x_recv_l[rd, k].astype(F32)
-        new = adagrad(left_t, left_s, total)
+        new = adagrad(left_t, left_s, left_finish())
         if not last:
             tab_l[rd + 1, mine] = new.astype(BF16)
             left_state = gather_left_start(rd + 1)
         else:
-            rel_step(3, rel_wait)
-            if len(dom_groups) > 1:
-                rel_wait = rel_start(4, 8, dom_groups[1])
-            left_out[...] = new.T
+            left_out[...] = new
             left_state_out[...] = left_s[...]
             to_owner.wait_recv()
             new = adagrad(right_t, right_s, y_recv[...])
-            right_out[...] = new.T
+            right_out[...] = new
             right_state_out[...] = right_s[...]
             if len(dom_groups) > 1:
                 rel_step(4, rel_wait)
@@ -408,6 +428,11 @@
 
     for copy in copies:
         copy.wait_send()
+
+
+def hand_out(*refs):
+    for source, target in zip(refs[:5], refs[5:]):
+        target[...] = source[...]
 
 
 def per_device(
@@ -422,15 +447,17 @@
     device_count = dom_size * lax.axis_size("row")
     rel_scale = (ROUNDS * edges * device_count) ** (-0.5)
     vmem = pltpu.VMEM
+    top = width // 2 // 16 * 16
+    shapes = (
+        jax.ShapeDtypeStruct((width, rows), F32),
+        jax.ShapeDtypeStruct((1, rows), F32),
+        jax.ShapeDtypeStruct((width, rows), F32),
+        jax.ShapeDtypeStruct((1, rows), F32),
+        jax.ShapeDtypeStruct((rels, width), F32),
+    )
     outs = pl.pallas_call(
         functools.partial(window_kernel, dom_size, rel_scale),
-        out_shape=(
-            jax.ShapeDtypeStruct((rows, width), F32),
-            jax.ShapeDtypeStruct((1, rows), F32),
-            jax.ShapeDtypeStruct((rows, width), F32),
-            jax.ShapeDtypeStruct((1, rows), F32),
-            jax.ShapeDtypeStruct((rels, width), F32),
-        ),
+        out_shape=shapes,
         in_specs=[pl.BlockSpec(memory_space=vmem)] * 9,
         out_specs=tuple([pl.BlockSpec(memory_space=vmem)] * 5),
         scratch_shapes=[
@@ -452,17 +479,17 @@
             vmem((2 * width, n_right), BF16),
             vmem((ROUNDS * 8, width, 2 * rows), F32),
             vmem((ROUNDS * 8, width, 2 * rows), F32),
-            vmem((ROUNDS, 3, width, 2 * rows), BF16),
-            vmem((ROUNDS, 3, width, 2 * rows), BF16),
-            vmem((ROUNDS, width, rows), BF16),
-            vmem((ROUNDS, width, rows), BF16),
             vmem((width, 2 * rows), F32),
-            vmem((ROUNDS, 3, width, rows), BF16),
-            vmem((ROUNDS, 3, width, rows), BF16),
-            vmem((ROUNDS, 4, width, rows), BF16),
-            vmem((ROUNDS, 4, width, rows), BF16),
-            vmem((4, width, rows), F32),
-            vmem((width, 2 * rows), F32),
+            vmem((ROUNDS * 2, 3, top, 2 * rows), BF16),
+            vmem((ROUNDS * 2, 3, top, 2 * rows), BF16),
+            vmem((ROUNDS * 2, top, rows), BF16),
+            vmem((ROUNDS * 2, top, rows), BF16),
+            vmem((2, top, 2 * rows), F32),
+            vmem((ROUNDS * 2, 4, width - top, rows), BF16),
+            vmem((ROUNDS * 2, 4, width - top, rows), BF16),
+            vmem((ROUNDS * 2, 3, width - top, rows), BF16),
+            vmem((ROUNDS * 2, 3, width - top, rows), BF16),
+            vmem((8, width - top, rows), F32),
             vmem((width, rows), BF16),
             vmem((width, rows), F32),
             vmem((width, rows), F32),
@@ -475,11 +502,16 @@
             collective_id=0, has_side_effects=True, vmem_limit_bytes=60 * 1024 * 1024
         ),
     )(
-        left_emb, left_state[None], right_emb, right_state[None], rel_diag,
+        left_emb.T, left_state[None], right_emb.T, right_state[None], rel_diag,
         edge_src, edge_rel, edge_dst, neg_rows.reshape(ROUNDS, negs),
     )
-    left_new, left_sum, right_new, right_sum, rel = outs
-    return left_new, left_sum.reshape(rows), right_new, right_sum.reshape(rows), rel
+    left_new, left_sum, right_new, right_sum, rel = pl.pallas_call(
+        hand_out,
+        out_shape=shapes,
+        in_specs=[pl.BlockSpec(memory_space=vmem)] * 5,
+        out_specs=tuple([pl.BlockSpec(memory_space=vmem)] * 5),
+    )(*outs)
+    return left_new.T, left_sum.reshape(rows), right_new.T, right_sum.reshape(rows), rel
 
 
 def solution(mesh):

time: 149 us -> 130 us (0.87); the launches traced: 149 us -> 128 us
  Pallas kernels: 141 us -> 127 us
  local copies, waits for them, and re-layouts: 7.01 us -> 0 us
    pallas_call x1, Pallas kernels: 141 us -> 125 us  [per_device(): pl.pallas_call(functools.partial(window_kernel, dom_size, rel_scale), out...]
    unnamed x17 -> x0, local copies, waits for them, and re-layouts: 7.01 us -> none
    pallas_call x0 -> x1, Pallas kernels: none -> 1.81 us  [per_device(): pl.pallas_call(hand_out, out_shape=shapes, in_specs=[pl.BlockSpec(memory_...]
where the time goes in v3:
time: 130 us; the launch traced here: 128 us
  Pallas kernels  127 us (98%)
    pallas_call x1, Pallas kernels, per_device(): pl.pallas_call(functools.partial(window_kernel, dom_size, rel_scale), out...  125 us

profile of v3, /device:TPU:24, one launch (start us, length us, event | category | flops | bytes accessed | tf_op | source)
XLA Modules:
  0.0 127.6 jit_solution(11753419985652931018)
XLA Ops:
  0.6 125.1 %shard_map.128 = (f32[400,128]{1,0:T(8,128)}, f32[1,128]{1,0:T(1,128)}, f32[400,128]{1,0:T(8,128)}, f32[1,128]{1,0:T(1,128)}, f32[16,400]{1,0:T(8,128)}) custom-call(f32[400,128]{1,0:T(8,128)} %bitcast.9, f32[1,128]{1,0:T(1,128)} %bitcast.12, f32[400,128]{1,0:T(8,128)} %bitcast.10, f32[1,128]{1,0:T(1,128)} %bitcast.13, f32[16,400]{1,0:T(8,128)} %rel_ref.1, ...), custom_call_target="tpu_custom_call" | custom-call | tf_op jit(solution)/shard_map/pallas_call | solution.py:458
  125.8 1.8 %shard_map.129 = (f32[400,128]{1,0:T(8,128)}, f32[1,128]{1,0:T(1,128)}, f32[400,128]{1,0:T(8,128)}, f32[1,128]{1,0:T(1,128)}, f32[16,400]{1,0:T(8,128)}) custom-call(f32[400,128]{1,0:T(8,128)} %get-tuple-element.15.refs_0_, f32[1,128]{1,0:T(1,128)} %get-tuple-element.16.refs_1_, f32[400,128]{1,0:T(8,128)} %get-tuple-element.17.refs_2_, ...), custom_call_target="tpu_custom_call" | custom-call | tf_op jit(solution)/shard_map/pallas_call | solution.py:508

commit v4 on v3

--- a/solution.py
+++ b/solution.py
@@ -37,7 +37,7 @@
     left_ref, left_state_ref, right_ref, right_state_ref, rel_ref, src_ref, relid_ref, dst_ref, neg_ref,
     left_out, left_state_out, right_out, right_state_out, rel_out,
     left_t, right_t, left_s, right_s, tab_l, tab_r, src_pos, right_pos,
-    rel_rows, left_rows, anchor, right_rows, right_tr, weights, src_hl, right_hl,
+    rel_rows, left_rows, anchor, right_rows, right_tr, weights, src_hl, right_hl, rel_hl,
     core_send, core_recv, unit_own,
     xa_send, xa_recv, za_send, za_recv, own_a, zb_send, zb_recv, xb_send, xb_recv, own_b, y_send, y_grad, y_recv,
     rel_part, rel_recv, send_sem, recv_sem,
@@ -119,14 +119,7 @@
                 got = got + out_ref[:, pl.ds(start, size)]
             out_ref[:, pl.ds(start, size)] = got
 
-        def body(t, carry):
-            tile(pl.multiple_of(t * 256, 256), 256)
-            return carry
-
-        count = ids_ref.shape[1]
-        lax.fori_loop(0, count // 256, body, 0)
-        if count % 256:
-            tile(count - count % 256, count % 256)
+        tile(0, ids_ref.shape[1])
 
     def pick_left(rd, core, first=False):
         stage("pick_left", lambda: pick_half(tab_l.at[rd], src_pos, left_rows, core, first))
@@ -134,10 +127,10 @@
     def pick_right(rd, core, first=False):
         stage("pick_right", lambda: pick_half(tab_r.at[rd], right_pos, right_rows, core, first))
 
-    def scatter_unit(hl_ref, ids_ref, core, xx):
+    def scatter_units(hl_ref, ids_ref, core, xs):
         sub = lax.broadcasted_iota(jnp.int32, (2 * rows, 1), 0)
-        base = core * 8 * rows + xx * 2 * rows
-        target = base + jnp.where(sub < rows, sub + (1 - z) * rows, sub - rows + z * rows)
+        inner = core * 8 * rows + jnp.where(sub < rows, sub + (1 - z) * rows, sub - rows + z * rows)
+        target = jnp.concatenate([inner + xx * 2 * rows for xx in xs], axis=0)
         hot = (target == ids_ref[...]).astype(F32).astype(BF16)
         both = dot(hl_ref[...], hot, NT)
         return both[:width] + both[width:]
@@ -163,7 +156,6 @@
     right_state = gather_right_start(0)
     left_state = gather_left_start(0)
 
-    rel_total = None
     for rd in range(ROUNDS):
         def indices():
             src_pos[...] = positions(src_ref[rd : rd + 1, :])
@@ -221,17 +213,17 @@
         stage("anchor", anchors)
 
         def score_tile(t, carry):
-            tile = pl.ds(pl.multiple_of(t * 256, 256), 256)
+            tile = pl.ds(pl.multiple_of(t * 512, 512), 512)
             scores = dot(right_tr[...], anchor[:, tile])
             weights[:, tile] = ((1.0 / (1.0 + jnp.exp(-scores))) * (1.0 / neg_count)).astype(BF16)
             scores = dot(right_tr[tile, :], anchor[:, tile])
-            eye = lax.broadcasted_iota(jnp.int32, (256, 256), 0) == lax.broadcasted_iota(jnp.int32, (256, 256), 1)
+            eye = lax.broadcasted_iota(jnp.int32, (512, 512), 0) == lax.broadcasted_iota(jnp.int32, (512, 512), 1)
             own = -1.0 / (1.0 + jnp.exp(scores))
             rest = weights[tile, tile].astype(F32)
             weights[tile, tile] = jnp.where(eye, own, rest).astype(BF16)
             return carry
 
-        stage("scores", lambda: lax.fori_loop(0, edges // 256, score_tile, 0))
+        stage("scores", lambda: lax.fori_loop(0, edges // 512, score_tile, 0))
 
         def grad_right(at, size):
             g = dot(anchor[...], weights[pl.ds(at, size), :], NT)
@@ -239,15 +231,7 @@
             right_hl[:width, pl.ds(at, size)] = high
             right_hl[width:, pl.ds(at, size)] = low
 
-        def grad_right_loop(t, carry):
-            grad_right(pl.multiple_of(t * 256, 256), 256)
-            return carry
-
-        def grad_right_all():
-            lax.fori_loop(0, edges // 256, grad_right_loop, 0)
-            grad_right(edges, negs)
-
-        stage("grad_right", grad_right_all)
+        stage("grad_right", lambda: grad_right(0, n_right))
 
         order = (2, 1, 3, 0)
 
@@ -256,28 +240,28 @@
 
             def partner(k):
                 def part():
-                    core_send[base + k] = scatter_unit(hl_ref, ids_ref, 1 - c, (x + order[k]) % 4)
+                    units = scatter_units(hl_ref, ids_ref, 1 - c, [(x + order[k + n]) % 4 for n in range(2)])
+                    core_send[base + k] = units[:, : 2 * rows]
+                    core_send[base + k + 1] = units[:, 2 * rows :]
 
                 stage(name, part)
-                sent[k] = send(core_send.at[base + k], core_recv.at[base + k], core_peer)
+                for n in (k, k + 1):
+                    sent[n] = send(core_send.at[base + n], core_recv.at[base + n], core_peer)
 
             def own(k):
                 def part():
-                    unit_own[...] = scatter_unit(hl_ref, ids_ref, c, (x + order[k]) % 4)
+                    unit_own[...] = scatter_units(hl_ref, ids_ref, c, [(x + order[k + n]) % 4 for n in range(2)])
 
                 stage(name, part)
-                sent[k].wait_recv()
-                use(k, unit_own[...] + core_recv[base + k])
+                for n in range(2):
+                    sent[k + n].wait_recv()
+                    use(k + n, unit_own[:, 2 * rows * n : 2 * rows * (n + 1)] + core_recv[base + k + n])
                 between(k)
 
             partner(0)
-            partner(1)
+            partner(2)
             own(0)
-            partner(2)
-            own(1)
-            partner(3)
             own(2)
-            own(3)
 
         def sums(side):
             at = rd * 2 + side
@@ -326,27 +310,24 @@
         left_use, left_on, left_top, left_finish = sums(1)
         scatter("scatter_right", right_hl, right_pos, rd * 8, right_use)
 
-        def grad_left_loop(t, acc):
-            at = pl.multiple_of(t * 256, 256)
-            tile = pl.ds(at, 256)
+        def grad_left_loop(t, carry):
+            tile = pl.ds(0, edges)
             g = dot(right_rows[...], weights[:, tile])
             high, low = split2(g * rel_rows[:, tile])
             src_hl[:width, tile] = high
             src_hl[width:, tile] = low
             high, low = split2(g * left_rows[:, tile].astype(F32))
-            hot = (
-                lax.broadcasted_iota(jnp.int32, (128, 256), 0) == relid_ref[rd : rd + 1, tile]
-            ).astype(F32)
-            hot = hot.astype(BF16)
-            return acc + dot(high, hot, NT) + dot(low, hot, NT)
-
-        def grad_left_all():
-            rel_acc = lax.fori_loop(0, edges // 256, grad_left_loop, jnp.zeros((width, 128), F32))
-            rel_part[5] = rel_acc.T[:rels]
-
-        stage("grad_left", grad_left_all)
-        rel_term = rel_part[5]
-        rel_total = rel_term if rel_total is None else rel_total + rel_term
+            rel_hl[:width, tile] = high
+            rel_hl[width:, tile] = low
+            return carry
+
+        stage("grad_left", lambda: grad_left_loop(0, 0))
+
+        def rel_sum():
+            hot = lax.broadcasted_iota(jnp.int32, (128, edges), 0) == relid_ref[rd : rd + 1, :]
+            both = dot(rel_hl[...], hot.astype(F32).astype(BF16), NT)
+            return (both[:width] + both[width:]).T[:rels]
+
         last = rd == ROUNDS - 1
         rel_wait = None
 
@@ -367,7 +348,7 @@
             rel_part[slot + 1] = total
 
         if last:
-            rel_part[0] = rel_total
+            rel_part[0] = rel_part[5] + rel_sum()
             rel_wait = rel_start(0, 0, {1: core_peer})
 
         right_on(0)
@@ -381,7 +362,7 @@
                 if last:
                     rel_step(0, rel_wait)
                     rel_wait = rel_start(1, 1, x_peers)
-            if k == 1:
+            if k == 2:
                 right_top()
 
         scatter("scatter_left", src_hl, src_pos, rd * 8 + 4, left_use, between)
@@ -389,6 +370,8 @@
         if last:
             rel_step(1, rel_wait)
             rel_wait = rel_start(2, 4, {1: z_peer})
+        else:
+            rel_part[5] = rel_sum()
         left_on(0)
         left_on(1)
         total = right_finish()
@@ -477,9 +460,10 @@
             vmem((n_right, edges), BF16),
             vmem((2 * width, edges), BF16),
             vmem((2 * width, n_right), BF16),
+            vmem((2 * width, edges), BF16),
             vmem((ROUNDS * 8, width, 2 * rows), F32),
             vmem((ROUNDS * 8, width, 2 * rows), F32),
-            vmem((width, 2 * rows), F32),
+            vmem((width, 4 * rows), F32),
             vmem((ROUNDS * 2, 3, top, 2 * rows), BF16),
             vmem((ROUNDS * 2, 3, top, 2 * rows), BF16),
             vmem((ROUNDS * 2, top, rows), BF16),

time: 130 us -> 117 us (0.900); the launches traced: 128 us -> 117 us
  Pallas kernels: 127 us -> 116 us
    pallas_call x1, Pallas kernels: 125 us -> 115 us  [per_device(): pl.pallas_call(functools.partial(window_kernel, dom_size, rel_scale), out...]
where the time goes in v4:
time: 117 us
  Pallas kernels  116 us (99%)
    pallas_call x1, Pallas kernels, per_device(): pl.pallas_call(functools.partial(window_kernel, dom_size, rel_scale), out...  115 us

profile of v4, /device:TPU:24, one launch (start us, length us, event | category | flops | bytes accessed | tf_op | source)
XLA Modules:
  0.0 117.0 jit_solution(13000120295066404950)
XLA Ops:
  0.6 114.6 %shard_map.128 = (f32[400,128]{1,0:T(8,128)}, f32[1,128]{1,0:T(1,128)}, f32[400,128]{1,0:T(8,128)}, f32[1,128]{1,0:T(1,128)}, f32[16,400]{1,0:T(8,128)}) custom-call(f32[400,128]{1,0:T(8,128)} %bitcast.9, f32[1,128]{1,0:T(1,128)} %bitcast.12, f32[400,128]{1,0:T(8,128)} %bitcast.10, f32[1,128]{1,0:T(1,128)} %bitcast.13, f32[16,400]{1,0:T(8,128)} %rel_ref.1, ...), custom_call_target="tpu_custom_call" | custom-call | tf_op jit(solution)/shard_map/pallas_call | solution.py:441
  115.2 1.8 %shard_map.129 = (f32[400,128]{1,0:T(8,128)}, f32[1,128]{1,0:T(1,128)}, f32[400,128]{1,0:T(8,128)}, f32[1,128]{1,0:T(1,128)}, f32[16,400]{1,0:T(8,128)}) custom-call(f32[400,128]{1,0:T(8,128)} %get-tuple-element.15.refs_0_, f32[1,128]{1,0:T(1,128)} %get-tuple-element.16.refs_1_, f32[400,128]{1,0:T(8,128)} %get-tuple-element.17.refs_2_, ...), custom_call_target="tpu_custom_call" | custom-call | tf_op jit(solution)/shard_map/pallas_call | solution.py:492

commit v5 on v4

--- a/solution.py
+++ b/solution.py
@@ -178,14 +178,25 @@
         right_x, right_z = right_state
         left_z, left_x = left_state
         left_cores, right_cores = {}, {}
-        left_z.wait_recv()
-        got = tab_l.at[rd, place(c, x, 1 - z)]
-        left_x2 = {dx: send(got, got, x_peers[dx]) for dx in (2, 1, 3)}
-        left_cores[0] = core_pair(tab_l.at[rd], x)
-        for dx in (1, 3, 2):
-            right_x[dx].wait_recv()
-            got = tab_r.at[rd, place(c, (x + 4 - dx) % 4, z)]
-            right_z[dx] = send(got, got, z_peer)
+
+        def left_forward():
+            left_z.wait_recv()
+            got = tab_l.at[rd, place(c, x, 1 - z)]
+            left_cores[0] = core_pair(tab_l.at[rd], x)
+            return {dx: send(got, got, x_peers[dx]) for dx in (2, 1, 3)}
+
+        def right_forward():
+            for dx in (1, 3, 2):
+                right_x[dx].wait_recv()
+                got = tab_r.at[rd, place(c, (x + 4 - dx) % 4, z)]
+                right_z[dx] = send(got, got, z_peer)
+
+        if rd == 0:
+            left_x2 = left_forward()
+            right_forward()
+        else:
+            right_forward()
+            left_x2 = left_forward()
         for dx in (0, 1, 3, 2):
             right_z[dx].wait_recv()
             right_cores[dx] = core_pair(tab_r.at[rd], (x + 4 - dx) % 4)
@@ -216,14 +227,18 @@
             tile = pl.ds(pl.multiple_of(t * 512, 512), 512)
             scores = dot(right_tr[...], anchor[:, tile])
             weights[:, tile] = ((1.0 / (1.0 + jnp.exp(-scores))) * (1.0 / neg_count)).astype(BF16)
-            scores = dot(right_tr[tile, :], anchor[:, tile])
-            eye = lax.broadcasted_iota(jnp.int32, (512, 512), 0) == lax.broadcasted_iota(jnp.int32, (512, 512), 1)
-            own = -1.0 / (1.0 + jnp.exp(scores))
-            rest = weights[tile, tile].astype(F32)
-            weights[tile, tile] = jnp.where(eye, own, rest).astype(BF16)
             return carry
 
-        stage("scores", lambda: lax.fori_loop(0, edges // 512, score_tile, 0))
+        def score_all():
+            lax.fori_loop(0, edges // 512, score_tile, 0)
+            products = anchor[...].astype(F32) * right_rows[:, :edges].astype(F32)
+            own = -1.0 / (1.0 + jnp.exp(jnp.sum(products, axis=0, keepdims=True)))
+            eye = lax.broadcasted_iota(jnp.int32, (128, 128), 0) == lax.broadcasted_iota(jnp.int32, (128, 128), 1)
+            for b in range(edges // 128):
+                tile = slice(b * 128, (b + 1) * 128)
+                weights[tile, tile] = jnp.where(eye, own[:, tile], weights[tile, tile].astype(F32)).astype(BF16)
+
+        stage("scores", score_all)
 
         def grad_right(at, size):
             g = dot(anchor[...], weights[pl.ds(at, size), :], NT)
@@ -329,14 +344,21 @@
             return (both[:width] + both[width:]).T[:rels]
 
         last = rd == ROUNDS - 1
-        rel_wait = None
-
-        def rel_start(slot, at, group):
-            return {j: (send(rel_part.at[slot], rel_recv.at[at + n], group[j]), at + n) for n, j in enumerate(group)}
-
-        def rel_step(slot, arriving):
+        rel_groups = [{1: core_peer}, *dom_groups, x_peers, {1: z_peer}]
+        rel_waits = []
+
+        def rel_start(slot):
+            at = sum(len(group) for group in rel_groups[:slot])
+            waiting = {}
+            for n, j in enumerate(rel_groups[slot]):
+                copy = send(rel_part.at[slot], rel_recv.at[at + n], rel_groups[slot][j])
+                waiting[j] = (copy, at + n)
+            rel_waits.append(waiting)
+
+        def rel_advance():
+            slot = len(rel_waits) - 1
             values = {}
-            for j, (copy, at) in arriving.items():
+            for j, (copy, at) in rel_waits[slot].items():
                 copy.wait_recv()
                 values[j] = rel_recv[at]
             own = rel_part[slot]
@@ -346,40 +368,36 @@
                 (only,) = values.values()
                 total = own + only
             rel_part[slot + 1] = total
+            if slot + 1 < len(rel_groups):
+                rel_start(slot + 1)
 
         if last:
             rel_part[0] = rel_part[5] + rel_sum()
-            rel_wait = rel_start(0, 0, {1: core_peer})
+            rel_start(0)
 
         right_on(0)
         right_on(1)
 
         def between(k):
-            nonlocal rel_wait
             if k == 0:
                 right_on(2)
                 right_on(3)
                 if last:
-                    rel_step(0, rel_wait)
-                    rel_wait = rel_start(1, 1, x_peers)
+                    rel_advance()
             if k == 2:
                 right_top()
 
         scatter("scatter_left", src_hl, src_pos, rd * 8 + 4, left_use, between)
 
         if last:
-            rel_step(1, rel_wait)
-            rel_wait = rel_start(2, 4, {1: z_peer})
-        else:
-            rel_part[5] = rel_sum()
+            rel_advance()
         left_on(0)
         left_on(1)
         total = right_finish()
         if last:
             y_grad[...] = total
             to_owner = send(y_grad, y_recv, y_peer)
-            rel_step(2, rel_wait)
-            rel_wait = rel_start(3, 5, dom_groups[0])
+            rel_advance()
         else:
             new = adagrad(right_t, right_s, total)
             y_send[...] = new.astype(BF16)
@@ -388,10 +406,9 @@
         left_on(3)
         left_top()
         if last:
-            rel_step(3, rel_wait)
-            if len(dom_groups) > 1:
-                rel_wait = rel_start(4, 8, dom_groups[1])
+            rel_advance()
         else:
+            rel_part[5] = rel_sum()
             to_holder.wait_recv()
             right_state = gather_right_start(rd + 1)
         new = adagrad(left_t, left_s, left_finish())
@@ -405,9 +422,9 @@
             new = adagrad(right_t, right_s, y_recv[...])
             right_out[...] = new
             right_state_out[...] = right_s[...]
-            if len(dom_groups) > 1:
-                rel_step(4, rel_wait)
-            rel_out[...] = rel_part[3 + len(dom_groups)] * rel_scale
+            if len(rel_groups) > 4:
+                rel_advance()
+            rel_out[...] = rel_part[len(rel_groups)] * rel_scale
 
     for copy in copies:
         copy.wait_send()

time: 117 us -> 115 us (0.983); the launches traced: 117 us -> 113 us
  Pallas kernels: 116 us -> 112 us
    pallas_call x1, Pallas kernels: 115 us -> 111 us  [per_device(): pl.pallas_call(functools.partial(window_kernel, dom_size, rel_scale), out...]
where the time goes in v5:
time: 115 us; the launch traced here: 113 us
  Pallas kernels  112 us (97%)
    pallas_call x1, Pallas kernels, per_device(): pl.pallas_call(functools.partial(window_kernel, dom_size, rel_scale), out...  111 us

profile of v5, /device:TPU:24, one launch (start us, length us, event | category | flops | bytes accessed | tf_op | source)
XLA Modules:
  0.0 113.1 jit_solution(9205545956890756645)
XLA Ops:
  0.6 110.7 %shard_map.128 = (f32[400,128]{1,0:T(8,128)}, f32[1,128]{1,0:T(1,128)}, f32[400,128]{1,0:T(8,128)}, f32[1,128]{1,0:T(1,128)}, f32[16,400]{1,0:T(8,128)}) custom-call(f32[400,128]{1,0:T(8,128)} %bitcast.9, f32[1,128]{1,0:T(1,128)} %bitcast.12, f32[400,128]{1,0:T(8,128)} %bitcast.10, f32[1,128]{1,0:T(1,128)} %bitcast.13, f32[16,400]{1,0:T(8,128)} %rel_ref.1, ...), custom_call_target="tpu_custom_call" | custom-call | tf_op jit(solution)/shard_map/pallas_call | solution.py:458
  111.3 1.8 %shard_map.129 = (f32[400,128]{1,0:T(8,128)}, f32[1,128]{1,0:T(1,128)}, f32[400,128]{1,0:T(8,128)}, f32[1,128]{1,0:T(1,128)}, f32[16,400]{1,0:T(8,128)}) custom-call(f32[400,128]{1,0:T(8,128)} %get-tuple-element.15.refs_0_, f32[1,128]{1,0:T(1,128)} %get-tuple-element.16.refs_1_, f32[400,128]{1,0:T(8,128)} %get-tuple-element.17.refs_2_, ...), custom_call_target="tpu_custom_call" | custom-call | tf_op jit(solution)/shard_map/pallas_call | solution.py:509
